TPU v7x, 32 devices: a whole 2x2x4 slice. The times are simulated.
32 devices in a mesh: groups: 2 (over x), tok: 16 (over z, y, core).
Axes of the slice: x: 2, y: 2, z: 4, core: 2. Of those that a mesh axis runs over, the one named last changes fastest.
Arguments:
- queries: bfloat16 [384, 32, 4096], P('tok', 'groups'), parts along dimension 1, may hold values from -32 to 32
- cross_query_rows: bfloat16 [384, 32, 4096], P('tok', 'groups'), parts along dimension 1, may hold values from -32 to 32
- prompt_key_rows: bfloat16 [384, 32, 512], P('tok', 'groups'), parts along dimension 1, may hold values from -32 to 32
- prompt_value_rows: bfloat16 [384, 32, 512], P('tok', 'groups'), parts along dimension 1, may hold values from -6 to 6
- image_cache: bfloat16 [2, 4, 512, 512], P(None, 'groups'), parts along dimension 1, may hold values from -32 to 32
- query_head_gate: float32 [32], replicated, may hold values from -2 to 2
- lengths: int32 [32], P('groups'), parts along dimension 0, may hold values from 1 to 384, 3072 in all
- owner_slot: int32 [32], P('groups'), parts along dimension 0, may hold values from 0 to 15, each once
- image_index: int32 [32], P('groups'), parts along dimension 0, may hold values from 0 to 1
Outputs:
- attended: bfloat16 [384, 32, 4096], P('tok', 'groups'), parts along dimension 1
- kv_cache: bfloat16 [2, 32, 384, 512], P(None, ('groups', 'tok')), parts along dimension 1
There are 2 independent parts, one for each index of `groups`. A program takes and returns all parts, laid end to end along the dimension named above; an argument that names none is the same for every part. Nothing has to cross between parts.
Inputs may be any that keep to these rules, and one draw needn't show every extreme that they name: `lengths`: some request has length 384. `owner_slot`: each slot owns exactly one request.
All inputs are finite; a program needn't handle non-finite values.
Results may differ from a plain program's by a relative error of at most 0.005.
Values may be sent and summed in bfloat16 or wider, within the bound.
A program may use at most 128 MiB of HBM per device.

v0:
```python
import math

import jax
import jax.numpy as jnp
from jax import lax
from jax.sharding import PartitionSpec as P

HQ = 32
KEY_HEAD_COUNT = 4
HEAD_WIDTH = 128
QUERY_PER_KEY = 8
SLOT_LENGTH = 384


def image_part(prompt_query_rows, image_row_block):
    count_of_rows = prompt_query_rows.shape[0]
    query_head_rows = prompt_query_rows.reshape(
        count_of_rows, KEY_HEAD_COUNT, QUERY_PER_KEY, HEAD_WIDTH
    )
    image_key_rows = image_row_block[0].reshape(-1, KEY_HEAD_COUNT, HEAD_WIDTH)
    image_value_rows = image_row_block[1].reshape(-1, KEY_HEAD_COUNT, HEAD_WIDTH)
    score_scale = 1.0 / math.sqrt(HEAD_WIDTH)

    def image_per_group(head_group):
        query_group = lax.dynamic_index_in_dim(query_head_rows, head_group, 1, keepdims=False)
        key_group = lax.dynamic_index_in_dim(image_key_rows, head_group, 1, keepdims=False)
        value_group = lax.dynamic_index_in_dim(image_value_rows, head_group, 1, keepdims=False)
        scores = (
            jnp.einsum("lqd,nd->lqn", query_group, key_group, preferred_element_type=jnp.float32)
            * score_scale
        )
        row_top = jnp.max(scores, axis=-1, keepdims=True)
        weights = jnp.exp(scores - row_top)
        row_total = jnp.sum(weights, axis=-1, keepdims=True)
        weighted = jnp.einsum(
            "lqn,nd->lqd",
            weights.astype(jnp.bfloat16),
            value_group,
            preferred_element_type=jnp.float32,
        )
        return weighted / row_total

    grouped_rows = lax.map(image_per_group, jnp.arange(KEY_HEAD_COUNT, dtype=jnp.int32))
    return jnp.transpose(grouped_rows, (1, 0, 2, 3))


def causal_part(owned_query_rows, owned_key_rows, owned_value_rows, block_count):
    query_head_rows = owned_query_rows.reshape(
        SLOT_LENGTH, KEY_HEAD_COUNT, QUERY_PER_KEY, HEAD_WIDTH
    )
    key_head_rows = owned_key_rows.reshape(SLOT_LENGTH, KEY_HEAD_COUNT, HEAD_WIDTH)
    value_head_rows = owned_value_rows.reshape(SLOT_LENGTH, KEY_HEAD_COUNT, HEAD_WIDTH)
    score_scale = 1.0 / math.sqrt(HEAD_WIDTH)
    block_rows = min(128, SLOT_LENGTH)
    positions = jnp.arange(SLOT_LENGTH, dtype=jnp.int32)

    def causal_per_group(head_group):
        query_group = lax.dynamic_index_in_dim(query_head_rows, head_group, 1, keepdims=False)
        key_group = lax.dynamic_index_in_dim(key_head_rows, head_group, 1, keepdims=False)
        value_group = lax.dynamic_index_in_dim(value_head_rows, head_group, 1, keepdims=False)

        def absorb(block_index, state):
            row_top, row_total, weighted = state
            offset = block_index * block_rows
            key_block = lax.dynamic_slice_in_dim(key_group, offset, block_rows, 0)
            value_block = lax.dynamic_slice_in_dim(value_group, offset, block_rows, 0)
            scores = (
                jnp.einsum(
                    "lqd,md->lqm", query_group, key_block, preferred_element_type=jnp.float32
                )
                * score_scale
            )
            key_positions = offset + jnp.arange(block_rows, dtype=jnp.int32)
            allowed = key_positions[None, :] <= positions[:, None]
            scores = jnp.where(allowed[:, None, :], scores, -1e30)
            new_top = jnp.maximum(row_top, jnp.max(scores, axis=-1))
            rescale = jnp.exp(row_top - new_top)
            weights = jnp.exp(scores - new_top[:, :, None])
            row_total = row_total * rescale + jnp.sum(weights, axis=-1)
            weighted = weighted * rescale[:, :, None] + jnp.einsum(
                "lqm,md->lqd",
                weights.astype(jnp.bfloat16),
                value_block,
                preferred_element_type=jnp.float32,
            )
            return (new_top, row_total, weighted)

        initial = (
            jnp.full((SLOT_LENGTH, QUERY_PER_KEY), -1e30, jnp.float32),
            jnp.zeros((SLOT_LENGTH, QUERY_PER_KEY), jnp.float32),
            jnp.zeros((SLOT_LENGTH, QUERY_PER_KEY, HEAD_WIDTH), jnp.float32),
        )
        row_top, row_total, weighted = lax.fori_loop(0, block_count, absorb, initial)
        return weighted / row_total[:, :, None]

    grouped_rows = lax.map(causal_per_group, jnp.arange(KEY_HEAD_COUNT, dtype=jnp.int32))
    return jnp.transpose(grouped_rows, (1, 0, 2, 3))


def shards(
    queries,
    cross_query_rows,
    prompt_key_rows,
    prompt_value_rows,
    image_cache,
    query_head_gate,
    lengths,
    owner_slot,
    image_index,
):
    devices = lax.axis_size("tok")
    my_rank = lax.axis_index("tok")
    slot_ids = jnp.arange(devices, dtype=jnp.int32)
    owned_mask = (owner_slot[:, None] == slot_ids[None, :]).astype(jnp.int32)
    slot_request = jnp.sum(slot_ids[:, None] * owned_mask, axis=0)
    own_request = lax.dynamic_index_in_dim(slot_request, my_rank, 0, keepdims=False)
    length = lax.dynamic_index_in_dim(lengths, own_request, 0, keepdims=False)
    picture = lax.dynamic_index_in_dim(image_index, own_request, 0, keepdims=False)
    image_row_block = lax.dynamic_index_in_dim(image_cache, picture, 1, keepdims=False)
    send_queries = jnp.take(queries, slot_request, axis=1)
    send_keys = jnp.take(prompt_key_rows, slot_request, axis=1)
    send_values = jnp.take(prompt_value_rows, slot_request, axis=1)
    squashed_gate = jnp.tanh(query_head_gate).reshape(KEY_HEAD_COUNT, QUERY_PER_KEY)
    block_rows = min(128, SLOT_LENGTH)
    block_count = SLOT_LENGTH // block_rows
    send_cross = jnp.take(cross_query_rows, slot_request, axis=1)
    owned_query_rows, own_cross, owned_key_rows, owned_value_rows = (
        lax.all_to_all(send_queries, "tok", split_axis=1, concat_axis=0, tiled=True),
        lax.all_to_all(send_cross, "tok", split_axis=1, concat_axis=0, tiled=True),
        lax.all_to_all(send_keys, "tok", split_axis=1, concat_axis=0, tiled=True),
        lax.all_to_all(send_values, "tok", split_axis=1, concat_axis=0, tiled=True),
    )
    cross_owned = image_part(own_cross.reshape(SLOT_LENGTH, HQ * HEAD_WIDTH), image_row_block)
    causal_out = causal_part(owned_query_rows, owned_key_rows, owned_value_rows, block_count)
    positions = jnp.arange(SLOT_LENGTH, dtype=jnp.int32)
    live_rows = positions < length
    self_rounded = lax.optimization_barrier(causal_out.astype(jnp.bfloat16))
    combined = self_rounded.astype(jnp.float32) + squashed_gate[None, :, :, None] * cross_owned
    combined = jnp.where(live_rows[:, None, None, None], combined, 0.0)
    outgoing = combined.reshape(SLOT_LENGTH, 1, HQ * HEAD_WIDTH).astype(jnp.bfloat16)
    returned = lax.all_to_all(outgoing, "tok", split_axis=0, concat_axis=1, tiled=True)
    arranged = jnp.take(returned, owner_slot, axis=1)
    zero_entry = jnp.zeros((), owned_key_rows.dtype)
    cache_keys = jnp.where(live_rows[:, None], owned_key_rows[:, 0, :], zero_entry)
    cache_values = jnp.where(live_rows[:, None], owned_value_rows[:, 0, :], zero_entry)
    kv_cache = jnp.stack([cache_keys, cache_values])[:, None]
    return (arranged, kv_cache)


def solution(mesh):
    placed = (
        P("tok", "groups", None),
        P("tok", "groups", None),
        P("tok", "groups", None),
        P("tok", "groups", None),
        P(None, "groups", None, None),
        P(),
        P("groups"),
        P("groups"),
        P("groups"),
    )
    return jax.shard_map(
        shards,
        mesh=mesh,
        in_specs=placed,
        out_specs=(P("tok", "groups", None), P(None, ("groups", "tok"), None, None)),
        check_vma=False,
    )
```

profile of v0, /device:TPU:31, one launch (start us, length us, event | category | flops | bytes accessed | tf_op | source)
XLA Modules:
  0.0 397.4 jit_solution(2211271806765260714)
XLA Ops:
  3.0 3.4 gather_fusion
  11.8 6.8 %all-to-all-start = ((bf16[24,16,512]{2,0,1:T(8,128)(2,1)}), bf16[24,16,512]{2,0,1:T(8,128)(2,1)S(1)}, u32[]{:S(2)}, u32[]{:S(2)}) async-start(bf16[24,16,512]{2,0,1:T(8,128)(2,1)} %copy.67), calls=%async_computation | async-start | bytes 786432 | tf_op jit(solution)/shard_map/all_to_all | solution.py:130
  18.6 11.2 %gather_fusion.2 = bf16[16,24,4096]{2,0,1:T(8,128)(2,1)} fusion(bf16[24,16,4096]{2,1,0:T(8,128)(2,1)S(1)} %copy-done, s32[1024]{0:T(1024)S(1)} %pad_clamp_fusion.1), kind=kCustom, calls=%fused_computation.clone | custom fusion | bytes 6291520 | tf_op jit(solution)/shard_map/jit(_take)/gather | solution.py:120
  29.8 9.8 %gather_fusion.3 = bf16[16,24,4096]{2,0,1:T(8,128)(2,1)} fusion(bf16[24,16,4096]{2,1,0:T(8,128)(2,1)} %param.20, s32[1024]{0:T(1024)S(1)} %pad_clamp_fusion.1), kind=kCustom, calls=%fused_computation.2.clone | custom fusion | bytes 6291520 | tf_op jit(solution)/shard_map/jit(_take)/gather | solution.py:126
  40.6 6.0 %all-to-all-start.1 = ((bf16[24,16,512]{2,0,1:T(8,128)(2,1)}), bf16[24,16,512]{2,0,1:T(8,128)(2,1)}, u32[]{:S(2)}, u32[]{:S(2)}) async-start(bf16[24,16,512]{2,0,1:T(8,128)(2,1)} %copy.68), calls=%async_computation.1 | async-start | bytes 786432 | tf_op jit(solution)/shard_map/all_to_all | solution.py:131
  46.6 5.1 %select_bitcast_fusion.2 = (bf16[24,16,4096]{2,1,0:T(8,128)(2,1)}, bf16[24,16,4096]{2,1,0:T(8,128)(2,1)S(1)}) fusion(bf16[16,24,4096]{2,0,1:T(8,128)(2,1)} %gather_fusion.2, pred[16]{0:T(512)(128)(4,1)S(1)} %get-tuple-element.379, bf16[16,24,4096]{2,0,1:T(8,128)(2,1)} %gather_fusion.3), kind=kLoop, calls=%fused_computation.55 | loop fusion | flops 3145728 | bytes 12582928 | tf_op jit(solution)/shard_map/jit(_take)/select_n | solution.py:120
  51.7 3.4 copy.74
  56.5 6.1 %all-to-all-start.3 = ((bf16[24,16,4096]{2,0,1:T(8,128)(2,1)}), bf16[24,16,4096]{2,0,1:T(8,128)(2,1)S(1)}, u32[]{:S(2)}, u32[]{:S(2)}) async-start(bf16[24,16,4096]{2,0,1:T(8,128)(2,1)} %copy.74), calls=%async_computation.3 | async-start | bytes 6291456 | tf_op jit(solution)/shard_map/all_to_all | solution.py:129
  74.1 5.3 %copy.69 = bf16[24,16,4096]{2,0,1:T(8,128)(2,1)} copy(bf16[24,16,4096]{2,1,0:T(8,128)(2,1)} %get-tuple-element.374) | data formatting | bytes 6291456 | tf_op jit(solution)/shard_map/jit(_take)/select_n | solution.py:120
  87.4 44.0 %all-to-all-done.3 = bf16[24,16,4096]{2,0,1:T(8,128)(2,1)S(1)} async-done(((bf16[24,16,4096]{2,0,1:T(8,128)(2,1)}), bf16[24,16,4096]{2,0,1:T(8,128)(2,1)S(1)}, u32[]{:S(2)}, u32[]{:S(2)}) %all-to-all-start.3) | async-done | bytes 3145760 | tf_op jit(solution)/shard_map/all_to_all | solution.py:129
  131.5 6.2 %all-to-all-start.2 = ((bf16[24,16,4096]{2,0,1:T(8,128)(2,1)}), bf16[24,16,4096]{2,0,1:T(8,128)(2,1)}, u32[]{:S(2)}, u32[]{:S(2)}) async-start(bf16[24,16,4096]{2,0,1:T(8,128)(2,1)} %copy.69), calls=%async_computation.2 | async-start | bytes 6291456 | tf_op jit(solution)/shard_map/all_to_all | solution.py:128
  137.7 2.5 copy.97
  140.2 46.4 %while.44 = (s32[]{:T(128)}, f32[4,384,8,128]{1,3,2,0:T(8,128)}, s32[4]{0:T(128)S(1)}, bf16[384,4,8,128]{3,2,1,0:T(8,128)(2,1)}, bf16[512,4,128]{0,2,1:T(8,128)(2,1)}, /*index=5*/bf16[512,4,128]{0,2,1:T(8,128)(2,1)}) while((s32[]{:T(128)}, f32[4,384,8,128]{1,3,2,0:T(8,128)}, s32[4]{0:T(128)S(1)}, ...), condition=%wide.region_10.13_spmd.clone, body=%wide.region_7.12_spmd.sunk.clone | while | flops 818276352 | bytes 29422208 | solution.py:43
  159.1 2.5 divide_bitcast_fusion.6
  170.7 2.5 divide_bitcast_fusion.6
  182.3 2.5 divide_bitcast_fusion.6
  186.6 20.0 %all-to-all-done.2 = bf16[24,16,4096]{2,0,1:T(8,128)(2,1)} async-done(((bf16[24,16,4096]{2,0,1:T(8,128)(2,1)}), bf16[24,16,4096]{2,0,1:T(8,128)(2,1)}, u32[]{:S(2)}, u32[]{:S(2)}) %all-to-all-start.2) | async-done | bytes 3145760 | tf_op jit(solution)/shard_map/all_to_all | solution.py:128
  206.6 4.4 %copy.96 = bf16[48,8,32,128]{3,2,1,0:T(8,128)(2,1)} copy(bf16[48,8,32,128]{3,1,2,0:T(8,128)(2,1)} %bitcast.61) | data formatting | bytes 6291456
  211.0 65.8 %while.46 = (s32[]{:T(128)}, bf16[4,384,8,128]{1,3,2,0:T(8,128)(2,1)}, s32[4]{0:T(128)S(1)}, bf16[384,4,128]{2,0,1:T(8,128)(2,1)}, bf16[384,4,128]{2,0,1:T(8,128...) while((s32[]{:T(128)}, ...), condition=%wide.region_6.9_spmd.clone.clone, body=%wide.region_1.8_spmd.clone.sunk.clone | while | flops 206109824 | bytes 18072516 | solution.py:96
  216.7 8.9 %while.45 = (s32[]{:T(128)}, f32[384,8]{0,1:T(8,128)S(1)}, f32[384,8]{0,1:T(8,128)S(1)}, f32[384,8,128]{2,0,1:T(8,128)S(1)}, s32[384]{0:T(512)S(1)}, /*index=5*/...) while((s32[]{:T(128)}, f32[384,8]{0,1:T(8,128)S(1)}, ...), condition=%wide.region_5.7_spmd.clone, body=%wide.region_2.6_spmd.clone.sunk | while | flops 205323392 | bytes 9013947 | solution.py:93
  233.1 8.9 %while.45 = (s32[]{:T(128)}, f32[384,8]{0,1:T(8,128)S(1)}, f32[384,8]{0,1:T(8,128)S(1)}, f32[384,8,128]{2,0,1:T(8,128)S(1)}, s32[384]{0:T(512)S(1)}, /*index=5*/...) while((s32[]{:T(128)}, f32[384,8]{0,1:T(8,128)S(1)}, ...), condition=%wide.region_5.7_spmd.clone, body=%wide.region_2.6_spmd.clone.sunk | while | flops 205323392 | bytes 9013947 | solution.py:93
  249.5 8.9 %while.45 = (s32[]{:T(128)}, f32[384,8]{0,1:T(8,128)S(1)}, f32[384,8]{0,1:T(8,128)S(1)}, f32[384,8,128]{2,0,1:T(8,128)S(1)}, s32[384]{0:T(512)S(1)}, /*index=5*/...) while((s32[]{:T(128)}, f32[384,8]{0,1:T(8,128)S(1)}, ...), condition=%wide.region_5.7_spmd.clone, body=%wide.region_2.6_spmd.clone.sunk | while | flops 205323392 | bytes 9013947 | solution.py:93
  266.0 8.9 %while.45 = (s32[]{:T(128)}, f32[384,8]{0,1:T(8,128)S(1)}, f32[384,8]{0,1:T(8,128)S(1)}, f32[384,8,128]{2,0,1:T(8,128)S(1)}, s32[384]{0:T(512)S(1)}, /*index=5*/...) while((s32[]{:T(128)}, f32[384,8]{0,1:T(8,128)S(1)}, ...), condition=%wide.region_5.7_spmd.clone, body=%wide.region_2.6_spmd.clone.sunk | while | flops 205323392 | bytes 9013947 | solution.py:93
  276.8 6.7 %fusion.31 = bf16[384,4,8,128]{0,3,2,1:T(8,128)(2,1)} fusion(f32[4,384,8,128]{1,3,2,0:T(8,128)} %get-tuple-element.214, bf16[384,4,8,128]{0,3,2,1:T(8,128)(2,1)} %bitcast.150, f32[4,8]{1,0:T(4,128)S(1)} %mul.70, pred[384]{0:T(512)(128)(4,1)S(1)} %iota_compare_fusion.1), kind=kLoop, calls=%fused_computation.52 | loop fusion | flops 7864320 | bytes 12583424 | tf_op jit(solution)/shard_map/convert_element_type | solution.py:140
  284.0 5.0 %reduce = bf16[384,4096]{0,1:T(8,128)(2,1)S(1)} reduce(bf16[384,1,4096]{0,2,1:T(8,128)(2,1)} %bitcast.151, bf16[]{:T(256)} %broadcast.261), dimensions={1}, to_apply=%copy.80.reduce_sub_computation | reduce | bytes 6291458 | tf_op jit(solution)/shard_map/convert_element_type | solution.py:140
  289.0 2.9 copy.104
  291.9 7.9 %reshape.211 = bf16[16,2,49152]{2,1,0:T(2,128)(2,1)} reshape(bf16[384,4096]{1,0:T(8,128)(2,1)} %copy.104) | data formatting | bytes 6291456
  299.8 6.3 %all-to-all-start.4 = ((bf16[16,2,49152]{2,1,0:T(2,128)(2,1)}), bf16[16,2,49152]{2,1,0:T(2,128)(2,1)S(1)}, u32[]{:S(2)}, u32[]{:S(2)}) async-start(bf16[16,2,49152]{2,1,0:T(2,128)(2,1)} %reshape.211), calls=%async_computation.4 | async-start | bytes 6291456 | tf_op jit(solution)/shard_map/all_to_all | solution.py:141
  308.3 66.7 %all-to-all-done.4 = bf16[16,2,49152]{2,1,0:T(2,128)(2,1)S(1)} async-done(((bf16[16,2,49152]{2,1,0:T(2,128)(2,1)}), bf16[16,2,49152]{2,1,0:T(2,128)(2,1)S(1)}, u32[]{:S(2)}, u32[]{:S(2)}) %all-to-all-start.4) | async-done | bytes 3145760 | tf_op jit(solution)/shard_map/all_to_all | solution.py:141
  375.0 7.6 %reshape.212 = bf16[384,1,4096]{2,1,0:T(2,128)(2,1)} reshape(bf16[16,2,49152]{2,1,0:T(2,128)(2,1)S(1)} %all-to-all-done.4) | data formatting | bytes 6291456
  382.6 6.3 %copy.92 = bf16[384,1,4096]{2,0,1:T(8,128)(2,1)S(1)} copy(bf16[384,1,4096]{2,1,0:T(2,128)(2,1)} %reshape.212) | data formatting | bytes 6291456
  393.8 3.4 copy.81
  (221 shorter events, 121.2 us)
Async XLA Ops:
  0.6 18.0 %copy-start = (bf16[24,16,4096]{2,1,0:T(8,128)(2,1)S(1)}, bf16[24,16,4096]{2,1,0:T(8,128)(2,1)}, u32[]{:S(2)}) copy-start(bf16[24,16,4096]{2,1,0:T(8,128)(2,1)} %param.19) | copy-start | bytes 9437188
  0.6 5.8 %copy-start.2 = (bf16[24,16,512]{2,1,0:T(8,128)(2,1)S(1)}, bf16[24,16,512]{2,1,0:T(8,128)(2,1)}, u32[]{:S(2)}) copy-start(bf16[24,16,512]{2,1,0:T(8,128)(2,1)} %param.22) | copy-start | bytes 1179652
  11.8 28.8 %all-to-all-start = ((bf16[24,16,512]{2,0,1:T(8,128)(2,1)}), bf16[24,16,512]{2,0,1:T(8,128)(2,1)S(1)}, u32[]{:S(2)}, u32[]{:S(2)}) async-start(bf16[24,16,512]{2,0,1:T(8,128)(2,1)} %copy.67), calls=%async_computation | async-start | bytes 786432 | tf_op jit(solution)/shard_map/all_to_all | solution.py:130
  29.8 9.8 %copy-start.5 = (bf16[24,16,512]{2,1,0:T(8,128)(2,1)S(1)}, bf16[24,16,512]{2,1,0:T(8,128)(2,1)}, u32[]{:S(2)}) copy-start(bf16[24,16,512]{2,1,0:T(8,128)(2,1)} %get-tuple-element.376) | copy-start | bytes 1179652
  40.6 42.3 %copy-start.3 = (bf16[24,16,512]{2,0,1:T(8,128)(2,1)}, bf16[24,16,512]{2,0,1:T(8,128)(2,1)S(1)}, u32[]{:S(2)}) copy-start(bf16[24,16,512]{2,0,1:T(8,128)(2,1)S(1)} %all-to-all-done) | copy-start | bytes 1179652
  40.6 16.0 %all-to-all-start.1 = ((bf16[24,16,512]{2,0,1:T(8,128)(2,1)}), bf16[24,16,512]{2,0,1:T(8,128)(2,1)}, u32[]{:S(2)}, u32[]{:S(2)}) async-start(bf16[24,16,512]{2,0,1:T(8,128)(2,1)} %copy.68), calls=%async_computation.1 | async-start | bytes 786432 | tf_op jit(solution)/shard_map/all_to_all | solution.py:131
  55.1 10.0 %copy-start.8 = (s32[16]{0:T(128)S(1)}, s32[16]{0:T(128)}, u32[]{:S(2)}) copy-start(s32[16]{0:T(128)} %param.27) | copy-start | bytes 196
  56.5 74.9 %all-to-all-start.3 = ((bf16[24,16,4096]{2,0,1:T(8,128)(2,1)}), bf16[24,16,4096]{2,0,1:T(8,128)(2,1)S(1)}, u32[]{:S(2)}, u32[]{:S(2)}) async-start(bf16[24,16,4096]{2,0,1:T(8,128)(2,1)} %copy.74), calls=%async_computation.3 | async-start | bytes 6291456 | tf_op jit(solution)/shard_map/all_to_all | solution.py:129
  74.1 5.3 %copy-start.9 = (s32[16]{0:T(128)S(1)}, s32[16]{0:T(128)}, u32[]{:S(2)}) copy-start(s32[16]{0:T(128)} %param.25) | copy-start | bytes 196
  74.1 5.9 %copy-start.10 = (f32[32]{0:T(128)S(1)}, f32[32]{0:T(128)}, u32[]{:S(2)}) copy-start(f32[32]{0:T(128)} %param.24) | copy-start | bytes 388
  131.5 75.1 %all-to-all-start.2 = ((bf16[24,16,4096]{2,0,1:T(8,128)(2,1)}), bf16[24,16,4096]{2,0,1:T(8,128)(2,1)}, u32[]{:S(2)}, u32[]{:S(2)}) async-start(bf16[24,16,4096]{2,0,1:T(8,128)(2,1)} %copy.69), calls=%async_computation.2 | async-start | bytes 6291456 | tf_op jit(solution)/shard_map/all_to_all | solution.py:128
  299.8 6.4 %copy-start.7 = (s32[16]{0:T(128)S(1)}, s32[16]{0:T(128)}, u32[]{:S(2)}) copy-start(s32[16]{0:T(128)} %param.26) | copy-start | bytes 196
  299.8 6.4 %copy-start.4 = (bf16[24,16,512]{2,0,1:T(8,128)(2,1)S(1)}, bf16[24,16,512]{2,0,1:T(8,128)(2,1)}, u32[]{:S(2)}) copy-start(bf16[24,16,512]{2,0,1:T(8,128)(2,1)} %copy-done.3) | copy-start | bytes 1179652
  299.8 75.2 %all-to-all-start.4 = ((bf16[16,2,49152]{2,1,0:T(2,128)(2,1)}), bf16[16,2,49152]{2,1,0:T(2,128)(2,1)S(1)}, u32[]{:S(2)}, u32[]{:S(2)}) async-start(bf16[16,2,49152]{2,1,0:T(2,128)(2,1)} %reshape.211), calls=%async_computation.4 | async-start | bytes 6291456 | tf_op jit(solution)/shard_map/all_to_all | solution.py:141
  388.9 2.4 copy-start.6
  391.4 5.8 %copy-start.1 = (bf16[24,16,4096]{2,1,0:T(8,128)(2,1)S(1)}, bf16[24,16,4096]{2,1,0:T(8,128)(2,1)}, u32[]{:S(2)}) copy-start(bf16[24,16,4096]{2,1,0:T(8,128)(2,1)} %param.19) | copy-start | bytes 9437188
where the time goes:
time: 404 us; the launch traced here: 397 us
  waiting for transfers between devices  132 us (33%)
  local copies, waits for them, and re-layouts  123 us (30%)
  matrix products  48.3 us (12%)
  other arithmetic  41.2 us (10%)
  starting transfers between devices  31.5 us (8%)
  loops' own time  16.6 us (4%)
  between operations  4.95 us (1%)
    all_to_all x1, waiting for transfers between devices, shards(): lax.all_to_all(outgoing, 'tok', split_axis=0, concat_axis=1, tiled=True)  66.7 us
    all_to_all x1, waiting for transfers between devices, shards(): lax.all_to_all(send_cross, 'tok', split_axis=1, concat_axis=0, tiled=True)  44 us
    unnamed x33, local copies, waits for them, and re-layouts  41.9 us
    all_to_all x1, waiting for transfers between devices, shards(): lax.all_to_all(send_queries, 'tok', split_axis=1, concat_axis=0, tiled=True)  20 us
    dot_general x12, matrix products, absorb(): jnp.einsum('lqd,md->lqm', query_group, key_block, preferred_element_type=...  18.6 us
    dynamic_update_slice x16, local copies, waits for them, and re-layouts, image_part(): lax.map(image_per_group, jnp.arange(KEY_HEAD_COUNT, dtype=jnp.int32))  12.5 us
    dot_general x12, matrix products, absorb(): jnp.einsum('lqm,md->lqd', weights.astype(jnp.bfloat16), value_block, pref...  11.9 us
    convert_element_type x2, other arithmetic, shards(): combined.reshape(SLOT_LENGTH, 1, HQ * HEAD_WIDTH).astype(jnp.bfloat16)  11.7 us
  transfers between devices with their start and end apart: 5, of which 4 were waited for; matrix products, arithmetic and copies ran while one was open for 24% of the time, Pallas kernels for 0%

commit v1 on v0

v1 whole, which is shorter than its diff:
```python
import functools
import math

import jax
import jax.numpy as jnp
from jax import lax
from jax.experimental import pallas as pl
from jax.experimental.pallas import tpu as pltpu
from jax.sharding import PartitionSpec as P

HQ = 32
KEY_HEAD_COUNT = 4
HEAD_WIDTH = 128
QUERY_PER_KEY = 8
SCALE = 1.0 / math.sqrt(HEAD_WIDTH)
VMEM_LIMIT = 48 * 1024 * 1024

NT = (((1,), (1,)), ((), ()))


def attend(queries, keys, values, bias):
    scores = lax.dot_general(queries, keys, NT, preferred_element_type=jnp.float32) * SCALE
    if bias is not None:
        scores = scores + bias
    top = jnp.max(scores, axis=-1, keepdims=True)
    weights = jnp.exp(scores - top)
    total = jnp.sum(weights, axis=-1, keepdims=True)
    weighted = jnp.dot(weights.astype(jnp.bfloat16), values, preferred_element_type=jnp.float32)
    return weighted, total


def cross_kernel(local, lengths_ref, image_ref, first_ref, query_ref, cache_ref, gate_ref, out_ref):
    request = pl.program_id(0)
    live = lengths_ref[request] > first_ref[0]

    @pl.when(live)
    def _():
        picture = image_ref[request]
        for group in range(KEY_HEAD_COUNT):
            lanes = slice(group * HEAD_WIDTH, (group + 1) * HEAD_WIDTH)
            weighted, total = attend(
                query_ref[0, group], cache_ref[0, picture, :, lanes], cache_ref[1, picture, :, lanes], None
            )
            out_ref[0, group] = (weighted * (gate_ref[group] / total)).astype(out_ref.dtype)

    @pl.when(jnp.logical_not(live))
    def _():
        out_ref[...] = jnp.zeros_like(out_ref)


def causal_kernel(local, slot, lengths_ref, first_ref, query_ref, kv_ref, cross_ref, out_ref):
    request = pl.program_id(0)
    first = first_ref[0]
    length = lengths_ref[request]
    live = length > first
    rows = QUERY_PER_KEY * local
    needed = first + local

    def run(keys):
        row = lax.broadcasted_iota(jnp.int32, (rows, keys), 0)
        position = first + lax.rem(row, local)
        key = lax.broadcasted_iota(jnp.int32, (rows, keys), 1)
        bias = jnp.where(key <= position, 0.0, -1e30)
        alive = position[:, :HEAD_WIDTH] < length
        for group in range(KEY_HEAD_COUNT):
            lanes = slice(group * HEAD_WIDTH, (group + 1) * HEAD_WIDTH)
            value_lanes = slice((KEY_HEAD_COUNT + group) * HEAD_WIDTH, (KEY_HEAD_COUNT + group + 1) * HEAD_WIDTH)
            weighted, total = attend(
                query_ref[0, group], kv_ref[0, :keys, lanes], kv_ref[0, :keys, value_lanes], bias
            )
            own = (weighted / total).astype(jnp.bfloat16).astype(jnp.float32)
            combined = own + cross_ref[0, group].astype(jnp.float32)
            out_ref[0, group] = jnp.where(alive, combined, 0.0).astype(out_ref.dtype)

    for keys in range(128, slot + 1, 128):
        @pl.when(live & (needed <= keys) & (needed > keys - 128))
        def _():
            run(keys)

    @pl.when(jnp.logical_not(live))
    def _():
        out_ref[...] = jnp.zeros_like(out_ref)


def shards(
    queries,
    cross_query_rows,
    prompt_key_rows,
    prompt_value_rows,
    image_cache,
    query_head_gate,
    lengths,
    owner_slot,
    image_index,
):
    local, requests, _ = queries.shape
    devices = lax.axis_size("tok")
    slot = local * devices
    rank = lax.axis_index("tok")
    rows = QUERY_PER_KEY * local
    first = jnp.full((1,), rank * local, jnp.int32)

    kv = jnp.concatenate([prompt_key_rows, prompt_value_rows], axis=-1)
    gathered = lax.all_gather(kv, "tok", axis=0, tiled=True)
    by_request = jnp.transpose(gathered, (1, 0, 2))

    def by_head(array):
        array = array.reshape(local, requests, KEY_HEAD_COUNT, QUERY_PER_KEY, HEAD_WIDTH)
        return jnp.transpose(array, (1, 2, 3, 0, 4)).reshape(requests, KEY_HEAD_COUNT, rows, HEAD_WIDTH)

    gate = jnp.tanh(query_head_gate).reshape(KEY_HEAD_COUNT, QUERY_PER_KEY, 1)
    gate = jnp.broadcast_to(gate, (KEY_HEAD_COUNT, QUERY_PER_KEY, local)).reshape(KEY_HEAD_COUNT, rows, 1)

    head_block = pl.BlockSpec((1, KEY_HEAD_COUNT, rows, HEAD_WIDTH), lambda r, *_: (r, 0, 0, 0))
    head_shape = jax.ShapeDtypeStruct((requests, KEY_HEAD_COUNT, rows, HEAD_WIDTH), jnp.bfloat16)
    params = pltpu.CompilerParams(vmem_limit_bytes=VMEM_LIMIT)
    flops = requests * HQ * local * HEAD_WIDTH * 4
    cross = pl.pallas_call(
        functools.partial(cross_kernel, local),
        grid_spec=pltpu.PrefetchScalarGridSpec(
            num_scalar_prefetch=3,
            grid=(requests,),
            in_specs=[
                head_block,
                pl.BlockSpec(image_cache.shape, lambda r, *_: (0, 0, 0, 0)),
                pl.BlockSpec(gate.shape, lambda r, *_: (0, 0, 0)),
            ],
            out_specs=head_block,
        ),
        out_shape=head_shape,
        compiler_params=params,
        cost_estimate=pl.CostEstimate(flops=flops * 512, bytes_accessed=8 << 20, transcendentals=0),
        name="cross",
    )(lengths, image_index, first, by_head(cross_query_rows), image_cache, gate)

    attended = pl.pallas_call(
        functools.partial(causal_kernel, local, slot),
        grid_spec=pltpu.PrefetchScalarGridSpec(
            num_scalar_prefetch=2,
            grid=(requests,),
            in_specs=[
                head_block,
                pl.BlockSpec((1, slot, 2 * KEY_HEAD_COUNT * HEAD_WIDTH), lambda r, *_: (r, 0, 0)),
                head_block,
            ],
            out_specs=head_block,
        ),
        out_shape=head_shape,
        compiler_params=params,
        cost_estimate=pl.CostEstimate(flops=flops * slot, bytes_accessed=24 << 20, transcendentals=0),
        name="causal",
    )(lengths, first, by_head(queries), by_request, cross)
    attended = attended.reshape(requests, KEY_HEAD_COUNT, QUERY_PER_KEY, local, HEAD_WIDTH)
    attended = jnp.transpose(attended, (3, 0, 1, 2, 4)).reshape(local, requests, HQ * HEAD_WIDTH)

    own_request = jnp.argmax(owner_slot == rank).astype(jnp.int32)
    length = lax.dynamic_index_in_dim(lengths, own_request, 0, keepdims=False)
    own = lax.dynamic_index_in_dim(by_request, own_request, 0, keepdims=False)
    own = jnp.where(jnp.arange(slot, dtype=jnp.int32)[:, None] < length, own, jnp.zeros((), own.dtype))
    width = KEY_HEAD_COUNT * HEAD_WIDTH
    kv_cache = jnp.stack([own[:, :width], own[:, width:]])[:, None]
    return attended, kv_cache


def solution(mesh):
    placed = (
        P("tok", "groups", None),
        P("tok", "groups", None),
        P("tok", "groups", None),
        P("tok", "groups", None),
        P(None, "groups", None, None),
        P(),
        P("groups"),
        P("groups"),
        P("groups"),
    )
    return jax.shard_map(
        shards,
        mesh=mesh,
        in_specs=placed,
        out_specs=(P("tok", "groups", None), P(None, ("groups", "tok"), None, None)),
        check_vma=False,
    )
```

time: 404 us -> 147 us (0.36)
  the two profiles are of different devices: /device:TPU:31 before, /device:TPU:0 now
where the time goes in v1:
time: 147 us
  waiting for transfers between devices  60.5 us (41%)
  Pallas kernels  43.5 us (30%)
  local copies, waits for them, and re-layouts  21.5 us (15%)
  between operations  16.3 us (11%)
  other arithmetic  4.73 us (3%)
    all_gather x1, waiting for transfers between devices, shards(): gathered = lax.all_gather(kv, 'tok', axis=0, tiled=True)  60.5 us
    pallas_call x1, Pallas kernels, shards(): pl.pallas_call(functools.partial(cross_kernel, local), grid_spec=pltpu.Pr...  24.5 us
    pallas_call x1, Pallas kernels, shards(): pl.pallas_call(functools.partial(causal_kernel, local, slot), grid_spec=p...  19 us
    reshape x2, local copies, waits for them, and re-layouts, by_head(): array.reshape(local, requests, KEY_HEAD_COUNT, QUERY_PER_KEY, HEAD_WIDTH)  10.6 us
    unnamed x20, local copies, waits for them, and re-layouts  5.95 us
    reshape x1, local copies, waits for them, and re-layouts, shards(): jnp.transpose(attended, (3, 0, 1, 2, 4))  3.31 us
  transfers between devices with their start and end apart: 1, of which 1 were waited for; matrix products, arithmetic and copies ran while one was open for 10% of the time, Pallas kernels for 17%

profile of v1, /device:TPU:0, one launch (start us, length us, event | category | flops | bytes accessed | tf_op | source)
XLA Modules:
  0.0 146.6 jit_solution(14187351268947423338)
XLA Ops:
  7.2 0.0 all-gather.2.cloned.1.call-start
  7.2 1.4 copy.18
  8.6 1.2 copy.17
  9.8 1.0 pad_maximum_fusion
  10.8 0.0 all-gather.2.cloned.1.call-update
  10.8 0.8 copy.22
  11.7 0.0 copy-start.5
  11.7 5.3 %copy.16 = bf16[24,16,4,8,128]{4,0,3,2,1:T(8,128)(2,1)} copy(bf16[24,16,4,8,128]{4,3,2,1,0:T(8,128)(2,1)S(1)} %bitcast.32) | data formatting | bytes 6291456 | tf_op jit(solution)/shard_map/reshape | solution.py:108
  17.0 0.0 copy-done.5
  17.0 0.8 copy.23
  17.8 0.0 copy-start.7
  17.9 0.0 copy-start.6
  17.9 0.0 copy-start.1
  17.9 0.0 copy-start.2
  17.9 0.0 copy-start.3
  17.9 5.3 %copy.19 = bf16[24,16,4,8,128]{4,0,3,2,1:T(8,128)(2,1)} copy(bf16[24,16,4,8,128]{4,3,2,1,0:T(8,128)(2,1)S(1)} %bitcast.33) | data formatting | bytes 6291456 | tf_op jit(solution)/shard_map/reshape | solution.py:108
  23.2 0.0 copy-done.7
  23.2 0.1 broadcast_in_dim.27
  23.3 0.1 broadcast_in_dim.28
  23.4 0.2 reshape.41.gate_ref
  23.6 0.9 compare_reduce_fusion
  26.6 0.6 dynamic_slice.6
  27.2 0.6 iota_compare_fusion
  27.8 24.5 %cross.1.cross_ref = bf16[16,4,192,128]{3,2,1,0:T(8,128)(2,1)S(1)} custom-call(s32[16]{0:T(128)S(1)} %copy-done.1, s32[16]{0:T(128)S(1)} %copy-done.3, s32[1]{0:T(128)} %bitcast.first_ref, bf16[16,4,192,128]{3,2,1,0:T(8,128)(2,1)} %bitcast.37, bf16[2,2,512,512]{3,2,1,0:T(8,128)(2,1)S(1)} %copy-done.2, f32[4,192,1]{2,1,0:T(8,128)S(1)} %reshape.41.gate_ref), custom_call_target="tpu_custom_call" | custom-call | flops 3221225472 | bytes 8388608 | tf_op jit(solution)/shard_map/cross/pallas_call | solution.py:118
  52.4 1.7 %copy-done = bf16[16,4,192,128]{3,2,1,0:T(8,128)(2,1)} copy-done((bf16[16,4,192,128]{3,2,1,0:T(8,128)(2,1)}, bf16[16,4,192,128]{3,2,1,0:T(8,128)(2,1)S(1)}, u32[]{:S(2)}) %copy-start) | copy-done | bytes 3145752
  54.0 60.5 %all-gather.2.cloned.1.call-done = bf16[384,16,1024]{2,0,1:T(8,128)(2,1)} async-done(((bf16[24,16,1024]{2,0,1:T(8,128)(2,1)}), bf16[384,16,1024]{2,0,1:T(8,128)(2,1)}) %all-gather.2.cloned.1.call-update) | async-done | bytes 12582928 | tf_op jit(solution)/shard_map/all_gather | solution.py:104
  114.5 19.0 %causal.1 = bf16[16,4,192,128]{3,2,1,0:T(8,128)(2,1)S(1)} custom-call(s32[16]{0:T(128)S(1)} %copy-done.1, s32[1]{0:T(128)} %bitcast.first_ref, bf16[16,4,192,128]{3,2,1,0:T(8,128)(2,1)} %bitcast.34, bf16[16,384,1024]{2,1,0:T(8,128)(2,1)} %bitcast.31, bf16[16,4,192,128]{3,2,1,0:T(8,128)(2,1)} %copy-done), custom_call_target="tpu_custom_call" | custom-call | flops 2415919104 | bytes 25165824 | tf_op jit(solution)/shard_map/causal/pallas_call | solution.py:136
  133.5 0.7 copy.21
  134.2 3.3 %reshape.40 = bf16[24,16,4096]{2,1,0:T(8,128)(2,1)} reshape(bf16[24,16,4,8,128]{4,3,2,1,0:T(8,128)(2,1)S(1)} %copy.21) | data formatting | bytes 6291456 | tf_op jit(solution)/shard_map/reshape | solution.py:154
  137.5 1.3 bitcast_select_fusion
  138.8 0.1 slice_bitcast_fusion.1
  138.8 0.9 maximum_bitcast_fusion
  (8 shorter events, 0.0 us)
Async XLA Ops:
  7.2 3.7 %copy-start.4 = (bf16[24,16,4096]{2,1,0:T(8,128)(2,1)S(1)}, bf16[24,16,4096]{2,1,0:T(8,128)(2,1)}, u32[]{:S(2)}) copy-start(bf16[24,16,4096]{2,1,0:T(8,128)(2,1)} %param.9) | copy-start | bytes 9437188
  7.2 107.3 %all-gather.2.cloned.1.call-start = ((), (), s32[]{:S(2)}) async-start(), calls=%async_computation | async-start | bytes 13369344 | tf_op jit(solution)/shard_map/all_gather | solution.py:104
  11.7 5.3 %copy-start.5 = (bf16[24,16,4096]{2,1,0:T(8,128)(2,1)S(1)}, bf16[24,16,4096]{2,1,0:T(8,128)(2,1)}, u32[]{:S(2)}) copy-start(bf16[24,16,4096]{2,1,0:T(8,128)(2,1)} %param.10) | copy-start | bytes 9437188
  17.8 5.4 %copy-start.7 = (f32[32]{0:T(128)S(1)}, f32[32]{0:T(128)}, u32[]{:S(2)}) copy-start(f32[32]{0:T(128)} %param.14) | copy-start | bytes 388
  17.9 5.7 %copy-start.6 = (s32[16]{0:T(128)S(1)}, s32[16]{0:T(128)}, u32[]{:S(2)}) copy-start(s32[16]{0:T(128)} %param.16) | copy-start | bytes 196
  17.9 8.7 %copy-start.1 = (s32[16]{0:T(128)S(1)}, s32[16]{0:T(128)}, u32[]{:S(2)}) copy-start(s32[16]{0:T(128)} %lengths_ref.3) | copy-start | bytes 196
  17.9 9.9 %copy-start.2 = (bf16[2,2,512,512]{3,2,1,0:T(8,128)(2,1)S(1)}, bf16[2,2,512,512]{3,2,1,0:T(8,128)(2,1)}, u32[]{:S(2)}) copy-start(bf16[2,2,512,512]{3,2,1,0:T(8,128)(2,1)} %cache_ref.1) | copy-start | bytes 6291460
  17.9 9.9 %copy-start.3 = (s32[16]{0:T(128)S(1)}, s32[16]{0:T(128)}, u32[]{:S(2)}) copy-start(s32[16]{0:T(128)} %image_ref.1) | copy-start | bytes 196
  52.3 1.7 %copy-start = (bf16[16,4,192,128]{3,2,1,0:T(8,128)(2,1)}, bf16[16,4,192,128]{3,2,1,0:T(8,128)(2,1)S(1)}, u32[]{:S(2)}) copy-start(bf16[16,4,192,128]{3,2,1,0:T(8,128)(2,1)S(1)} %cross.1.cross_ref) | copy-start | bytes 9437188
Sparse Core Ops, SparseCore 0:
  10.9 103.4 all-gather.1

commit v2 on v1

--- a/solution.py
+++ b/solution.py
@@ -162,6 +162,322 @@
     return attended, kv_cache
 
 
+CHUNK = 8
+
+
+def rank_limit(requests, slot, first):
+    if first == 0:
+        return requests
+    return min(requests, (requests * slot // 2 - requests) // first)
+
+
+def relay_plan(chips, requests, slot, step_us):
+    span = slot // chips
+    limit = [rank_limit(requests, slot, span * chip) for chip in range(chips)]
+    chunks = [(0, CHUNK), (CHUNK, requests)]
+
+    def ranks(chip, chunk, up):
+        lo, hi = chunks[chunk]
+        top = limit[chip - chip % 2] if up else limit[chip]
+        return lo, max(lo, min(hi, top))
+
+    free = {}
+    pending = [(0.0, chip, chip, "own", chunk) for chip in range(chips) for chunk in range(2)]
+    events = [[] for _ in range(chips)]
+    rate = span // 2 * 2048 / 45000.0
+    while pending:
+        pending.sort()
+        time, chip, source, via, chunk = pending.pop(0)
+        sends = []
+        if via != "side":
+            if chip + 2 < chips:
+                sends.append((chip + 2, "up"))
+            if source < (chip ^ 1):
+                sends.append((chip ^ 1, "side"))
+        kept = []
+        for target, way in sends:
+            lo, hi = ranks(target, chunk, way == "up")
+            if hi > lo:
+                start = max(time, free.get((chip, target), 0.0))
+                end = start + rate * (hi - lo)
+                free[chip, target] = end
+                pending.append((end + 1.0, target, source, way, chunk))
+                kept.append((target, lo, hi))
+        got = ranks(chip, chunk, via == "up")
+        need = ranks(chip, chunk, False)
+        events[chip].append((int(time / step_us), source, via, chunk, got, need, kept))
+    return events
+
+
+def gather_kernel(
+    devices, requests, local, plan, image_ref, picks_ref, query_ref, cache_ref, gate_ref,
+    kv_ref, owned_ref, cross_ref, send_sem, recv_sem, pass_sem, owned_send, owned_recv, local_sem,
+):
+    me = lax.axis_index("tok")
+    chip, core = lax.div(me, 2), lax.rem(me, 2)
+
+    barrier = pltpu.get_barrier_semaphore()
+
+    def greet(offset, carry):
+        pl.semaphore_signal(
+            barrier, inc=1, device_id={"tok": lax.rem(me + offset, devices)}, device_id_type=pl.DeviceIdType.MESH
+        )
+        return carry
+
+    lax.fori_loop(1, devices, greet, 0)
+    pl.semaphore_wait(barrier, devices - 1)
+
+    keep = pltpu.make_async_copy(picks_ref.at[pl.ds(0, requests)], kv_ref.at[me], local_sem.at[0])
+    keep_owned = pltpu.make_async_copy(picks_ref.at[requests + me], owned_ref.at[me], local_sem.at[1])
+    keep.start()
+    keep_owned.start()
+
+    def block(source, lo, hi, own):
+        if own:
+            return picks_ref.at[pl.ds(lo, hi - lo)]
+        return kv_ref.at[source, pl.ds(lo, hi - lo)]
+
+    def relay(source, lo, hi, chunk, target, send, own):
+        return pltpu.make_async_remote_copy(
+            src_ref=block(source, lo, hi, own),
+            dst_ref=kv_ref.at[source, pl.ds(lo, hi - lo)],
+            send_sem=send,
+            recv_sem=recv_sem.at[2 * source + chunk],
+            device_id={"tok": target},
+            device_id_type=pl.DeviceIdType.MESH,
+        )
+
+    def copies(number, position):
+        _, source_chip, via, chunk, _, need, sends = plan[number][position]
+        source = 2 * source_chip + core
+        result = []
+        for index, (target, lo, hi) in enumerate(sends):
+            result.append(
+                relay(source, lo, hi, chunk, 2 * target + core, send_sem.at[index, 2 * source_chip + chunk], via == "own")
+            )
+        if need[1] > need[0]:
+            result.append(
+                relay(source, need[0], need[1], chunk, 2 * number + 1 - core, pass_sem.at[2 * source_chip + chunk], via == "own")
+            )
+        return result
+
+    def handle(number, position):
+        _, source_chip, via, chunk, got, _, _ = plan[number][position]
+        source = 2 * source_chip + core
+        if via != "own":
+            relay(source, got[0], got[1], chunk, me, pass_sem.at[0], False).wait_recv()
+        for copy in copies(number, position):
+            copy.start()
+
+    def owned_copy(offset):
+        target = lax.rem(me + offset, devices)
+        return pltpu.make_async_remote_copy(
+            src_ref=picks_ref.at[requests + target],
+            dst_ref=owned_ref.at[me],
+            send_sem=owned_send.at[offset],
+            recv_sem=owned_recv.at[offset],
+            device_id={"tok": target},
+            device_id_type=pl.DeviceIdType.MESH,
+        )
+
+    def owned_start(offset, carry):
+        owned_copy(offset).start()
+        return carry
+
+    def step(request, carry):
+        for number in range(devices // 2):
+            @pl.when(chip == number)
+            def _():
+                for when in sorted({event[0] for event in plan[number] if event[0] < requests}):
+                    @pl.when(request == when)
+                    def _():
+                        for position, event in enumerate(plan[number]):
+                            if event[0] == when:
+                                handle(number, position)
+
+        @pl.when(request == 0)
+        def _():
+            lax.fori_loop(1, devices, owned_start, 0)
+
+        picture = image_ref[request]
+        for group in range(KEY_HEAD_COUNT):
+            lanes = slice(group * HEAD_WIDTH, (group + 1) * HEAD_WIDTH)
+            weighted, total = attend(
+                query_ref[request, group], cache_ref[0, picture, :, lanes], cache_ref[1, picture, :, lanes], None
+            )
+            cross_ref[request, group] = (weighted * (gate_ref[group] / total)).astype(cross_ref.dtype)
+        return carry
+
+    lax.fori_loop(0, requests, step, 0)
+
+    for number in range(devices // 2):
+        @pl.when(chip == number)
+        def _():
+            for position, event in enumerate(plan[number]):
+                if event[0] >= requests:
+                    handle(number, position)
+            for position, event in enumerate(plan[number]):
+                _, source_chip, _, chunk, _, need, _ = event
+                if need[1] > need[0]:
+                    relay(
+                        2 * source_chip + 1 - core, need[0], need[1], chunk, me, pass_sem.at[0], False
+                    ).wait_recv()
+                for copy in copies(number, position):
+                    copy.wait_send()
+
+    def owned_wait(offset, carry):
+        source = lax.rem(me + devices - offset, devices)
+        pltpu.make_async_remote_copy(
+            src_ref=picks_ref.at[requests + me],
+            dst_ref=owned_ref.at[source],
+            send_sem=owned_send.at[offset],
+            recv_sem=owned_recv.at[offset],
+            device_id={"tok": source},
+            device_id_type=pl.DeviceIdType.MESH,
+        ).wait_recv()
+        owned_copy(offset).wait_send()
+        return carry
+
+    lax.fori_loop(1, devices, owned_wait, 0)
+    keep.wait()
+    keep_owned.wait()
+
+
+def relayed_causal_kernel(local, slot, lengths_ref, rank_ref, first_ref, query_ref, kv_ref, cross_ref, out_ref):
+    request = pl.program_id(0)
+    first = first_ref[0]
+    length = lengths_ref[request]
+    live = length > first
+    rows = QUERY_PER_KEY * local
+    needed = first + local
+
+    def run(keys):
+        sources = -(-keys // local)
+        row = lax.broadcasted_iota(jnp.int32, (rows, keys), 0)
+        position = first + lax.rem(row, local)
+        key = lax.broadcasted_iota(jnp.int32, (rows, keys), 1)
+        allowed = key <= position
+        alive = position[:, :HEAD_WIDTH] < length
+        written = lax.broadcasted_iota(jnp.int32, (keys, HEAD_WIDTH), 0) < needed
+
+        def rows_of(lane_block):
+            lanes = slice(lane_block * HEAD_WIDTH, (lane_block + 1) * HEAD_WIDTH)
+            pieces = kv_ref[:sources, 0, :, lanes].astype(jnp.float32)
+            return pieces.reshape(sources * local, HEAD_WIDTH)[:keys]
+
+        for group in range(KEY_HEAD_COUNT):
+            key_rows = rows_of(group).astype(jnp.bfloat16)
+            value_rows = jnp.where(written, rows_of(KEY_HEAD_COUNT + group), 0.0).astype(jnp.bfloat16)
+            scores = lax.dot_general(query_ref[0, group], key_rows, NT, preferred_element_type=jnp.float32) * SCALE
+            scores = jnp.where(allowed, scores, -1e30)
+            top = jnp.max(scores, axis=-1, keepdims=True)
+            weights = jnp.exp(scores - top)
+            total = jnp.sum(weights, axis=-1, keepdims=True)
+            weighted = jnp.dot(weights.astype(jnp.bfloat16), value_rows, preferred_element_type=jnp.float32)
+            own = (weighted / total).astype(jnp.bfloat16).astype(jnp.float32)
+            combined = own + cross_ref[0, group].astype(jnp.float32)
+            out_ref[0, group] = jnp.where(alive, combined, 0.0).astype(out_ref.dtype)
+
+    for keys in range(128, slot + 1, 128):
+        @pl.when(live & (needed <= keys) & (needed > keys - 128))
+        def _():
+            run(keys)
+
+    @pl.when(jnp.logical_not(live))
+    def _():
+        out_ref[...] = jnp.zeros_like(out_ref)
+
+
+def relayed(
+    queries,
+    cross_query_rows,
+    prompt_key_rows,
+    prompt_value_rows,
+    image_cache,
+    query_head_gate,
+    lengths,
+    owner_slot,
+    image_index,
+):
+    local, requests, _ = queries.shape
+    devices = lax.axis_size("tok")
+    slot = local * devices
+    rank = lax.axis_index("tok")
+    rows = QUERY_PER_KEY * local
+    width = 2 * KEY_HEAD_COUNT * HEAD_WIDTH
+    first = jnp.full((1,), rank * local, jnp.int32)
+    ids = jnp.arange(requests, dtype=jnp.int32)
+
+    longer = lengths[None, :] > lengths[:, None]
+    tied = (lengths[None, :] == lengths[:, None]) & (ids[None, :] < ids[:, None])
+    length_rank = jnp.sum((longer | tied).astype(jnp.int32), axis=1)
+    chosen = jnp.concatenate([length_rank, owner_slot + requests]).reshape(2, requests)
+    places = jnp.arange(2 * requests, dtype=jnp.int32)
+    pick = (places[:, None, None] == chosen[None]).any(axis=1).astype(jnp.bfloat16)
+    kv = jnp.concatenate([prompt_key_rows, prompt_value_rows], axis=-1)
+    picks = jnp.einsum("sr,lrd->sld", pick, kv, preferred_element_type=jnp.float32).astype(jnp.bfloat16)
+
+    def by_head(array):
+        array = array.reshape(local, requests, KEY_HEAD_COUNT, QUERY_PER_KEY, HEAD_WIDTH)
+        return jnp.transpose(array, (1, 2, 3, 0, 4)).reshape(requests, KEY_HEAD_COUNT, rows, HEAD_WIDTH)
+
+    gate = jnp.tanh(query_head_gate).reshape(KEY_HEAD_COUNT, QUERY_PER_KEY, 1)
+    gate = jnp.broadcast_to(gate, (KEY_HEAD_COUNT, QUERY_PER_KEY, local)).reshape(KEY_HEAD_COUNT, rows, 1)
+
+    head_shape = jax.ShapeDtypeStruct((requests, KEY_HEAD_COUNT, rows, HEAD_WIDTH), jnp.bfloat16)
+    anywhere = pl.BlockSpec(memory_space=pl.ANY)
+    vmem = pl.BlockSpec(memory_space=pltpu.VMEM)
+    plan = relay_plan(devices // 2, requests, slot, 1.5)
+    kv_all, owned, cross = pl.pallas_call(
+        functools.partial(gather_kernel, devices, requests, local, plan),
+        in_specs=[pl.BlockSpec(memory_space=pltpu.SMEM), anywhere, vmem, vmem, vmem],
+        out_specs=[anywhere, anywhere, vmem],
+        out_shape=[
+            jax.ShapeDtypeStruct((devices, requests, local, width), jnp.bfloat16),
+            jax.ShapeDtypeStruct((devices, local, width), jnp.bfloat16),
+            head_shape,
+        ],
+        scratch_shapes=[
+            pltpu.SemaphoreType.DMA((2, devices)),
+            pltpu.SemaphoreType.DMA((2 * devices,)),
+            pltpu.SemaphoreType.DMA((devices,)),
+            pltpu.SemaphoreType.DMA((devices,)),
+            pltpu.SemaphoreType.DMA((devices,)),
+            pltpu.SemaphoreType.DMA((2,)),
+        ],
+        compiler_params=pltpu.CompilerParams(
+            collective_id=0, has_side_effects=True, vmem_limit_bytes=VMEM_LIMIT
+        ),
+        name="gather_cross",
+    )(image_index, picks, by_head(cross_query_rows), image_cache, gate)
+
+    head_block = pl.BlockSpec((1, KEY_HEAD_COUNT, rows, HEAD_WIDTH), lambda r, *_: (r, 0, 0, 0))
+    attended = pl.pallas_call(
+        functools.partial(relayed_causal_kernel, local, slot),
+        grid_spec=pltpu.PrefetchScalarGridSpec(
+            num_scalar_prefetch=3,
+            grid=(requests,),
+            in_specs=[
+                head_block,
+                pl.BlockSpec((devices, 1, local, width), lambda r, lengths, ranks, first: (0, ranks[r], 0, 0)),
+                head_block,
+            ],
+            out_specs=head_block,
+        ),
+        out_shape=head_shape,
+        compiler_params=pltpu.CompilerParams(vmem_limit_bytes=VMEM_LIMIT),
+        name="causal",
+    )(lengths, length_rank, first, by_head(queries), kv_all, cross)
+    attended = attended.reshape(requests, KEY_HEAD_COUNT, QUERY_PER_KEY, local, HEAD_WIDTH)
+    attended = jnp.transpose(attended, (3, 0, 1, 2, 4)).reshape(local, requests, HQ * HEAD_WIDTH)
+
+    length = jnp.sum(jnp.where(owner_slot == rank, lengths, 0))
+    own = owned.reshape(slot, width)
+    own = jnp.where(jnp.arange(slot, dtype=jnp.int32)[:, None] < length, own, jnp.zeros((), own.dtype))
+    kv_cache = jnp.stack([own[:, : width // 2], own[:, width // 2 :]])[:, None]
+    return attended, kv_cache
+
+
 def solution(mesh):
     placed = (
         P("tok", "groups", None),
@@ -175,7 +491,7 @@
         P("groups"),
     )
     return jax.shard_map(
-        shards,
+        relayed if mesh.shape["tok"] == 16 else shards,
         mesh=mesh,
         in_specs=placed,
         out_specs=(P("tok", "groups", None), P(None, ("groups", "tok"), None, None)),

time: 147 us -> 116 us (0.79)
  the two profiles are of different devices: /device:TPU:0 before, /device:TPU:31 now
where the time goes in v2:
time: 116 us; the launch traced here: 114 us
  Pallas kernels  87.5 us (75%)
  local copies, waits for them, and re-layouts  19.2 us (17%)
  other arithmetic  4.29 us (4%)
  matrix products  1.87 us (2%)
    pallas_call x1, Pallas kernels, relayed(): pl.pallas_call(functools.partial(gather_kernel, devices, requests, local,...  72.2 us
    pallas_call x1, Pallas kernels, relayed(): pl.pallas_call(functools.partial(relayed_causal_kernel, local, slot), gri...  15.2 us
    reshape x2, local copies, waits for them, and re-layouts, by_head(): array.reshape(local, requests, KEY_HEAD_COUNT, QUERY_PER_KEY, HEAD_WIDTH)  10.6 us
    reshape x1, local copies, waits for them, and re-layouts, relayed(): jnp.transpose(attended, (3, 0, 1, 2, 4))  3.31 us
    unnamed x14, local copies, waits for them, and re-layouts  3.28 us

profile of v2, /device:TPU:31, one launch (start us, length us, event | category | flops | bytes accessed | tf_op | source)
XLA Modules:
  0.0 113.6 jit_solution(10505489521413729173)
XLA Ops:
  0.6 1.3 %fusion.8 = (s32[]{:T(128)}, s32[16]{0:T(128)S(1)}) fusion(s32[16]{0:T(128)} %lengths_ref.1, s32[16]{0:T(128)} %param.16, s32[]{:T(128)S(6)} %axis_index.12), kind=kLoop, calls=%fused_computation.18 | loop fusion | flops 63 | bytes 200 | tf_op jit(solution)/shard_map/reduce_sum | solution.py:474
  1.9 0.9 convert_reduce_fusion.rank_ref
  2.9 0.1 pad_add_fusion
  2.9 0.1 eq.32
  3.0 0.1 fusion.4
  3.1 1.9 %fusion = bf16[32,24,1024]{2,0,1:T(8,128)(2,1)S(1)} fusion(bf16[24,16,512]{2,1,0:T(8,128)(2,1)} %param.12, bf16[24,16,512]{2,1,0:T(8,128)(2,1)} %param.11, pred[32,16]{0,1:T(8,128)(4,1)S(1)} %fusion.4), kind=kOutput, calls=%fused_computation.1 | convolution fusion | flops 26738688 | bytes 2359808 | tf_op jit(solution)/shard_map/sr,lrd->sld/dot_general | solution.py:418
  5.0 0.9 copy.28.picks_ref
  5.8 0.0 copy-done.3
  5.9 0.8 copy.26
  6.7 0.0 copy-start.5
  6.7 0.0 copy-start.2
  6.7 5.3 %copy.22 = bf16[24,16,4,8,128]{4,0,3,2,1:T(8,128)(2,1)} copy(bf16[24,16,4,8,128]{4,3,2,1,0:T(8,128)(2,1)S(1)} %bitcast.34) | data formatting | bytes 6291456 | tf_op jit(solution)/shard_map/reshape | solution.py:421
  12.0 0.0 copy-done.5
  12.0 0.1 broadcast_in_dim.38
  12.1 0.1 broadcast_in_dim.39
  12.2 0.2 reshape.47.gate_ref
  12.4 0.0 copy-done.2
  12.4 0.0 copy-start
  12.4 1.6 %copy-done = bf16[2,2,512,512]{3,2,1,0:T(8,128)(2,1)S(1)} copy-done((bf16[2,2,512,512]{3,2,1,0:T(8,128)(2,1)S(1)}, bf16[2,2,512,512]{3,2,1,0:T(8,128)(2,1)}, u32[]{:S(2)}) %copy-start) | copy-done | bytes 2097176
  14.0 72.2 %gather_cross.1 = (bf16[16,16,24,1024]{3,2,1,0:T(8,128)(2,1)}, bf16[16,24,1024]{2,1,0:T(8,128)(2,1)S(1)}, bf16[16,4,192,128]{3,2,1,0:T(8,128)(2,1)}) custom-call(s32[16]{0:T(128)S(1)} %copy-done.2, bf16[32,24,1024]{2,1,0:T(8,128)(2,1)S(1)} %copy.28.picks_ref, bf16[16,4,192,128]{3,2,1,0:T(8,128)(2,1)} %bitcast.32, bf16[2,2,512,512]{3,2,1,0:T(8,128)(2,1)S(1)} %copy-done, ...), custom_call_target="tpu_custom_call" | custom-call | tf_op jit(solution)/shard_map/gather_cross/pallas_call | solution.py:431
  86.2 0.0 copy-start.4
  86.3 0.8 iota_compare_fusion.2
  87.1 0.2 bitcast_select_fusion
  87.2 0.1 slice_bitcast_fusion.1
  87.3 0.9 maximum_bitcast_fusion
  88.2 0.0 copy-done.4
  88.2 0.8 copy.25
  89.1 0.0 copy-start.1
  89.1 5.3 %copy.20 = bf16[24,16,4,8,128]{4,0,3,2,1:T(8,128)(2,1)} copy(bf16[24,16,4,8,128]{4,3,2,1,0:T(8,128)(2,1)S(1)} %bitcast.35) | data formatting | bytes 6291456 | tf_op jit(solution)/shard_map/reshape | solution.py:421
  94.4 15.2 %causal.1 = bf16[16,4,192,128]{3,2,1,0:T(8,128)(2,1)S(1)} custom-call(s32[16]{0:T(128)S(1)} %copy-done.1, s32[16]{0:T(128)S(1)} %convert_reduce_fusion.rank_ref, s32[1]{0:T(128)} %bitcast.first_ref, bf16[16,4,192,128]{3,2,1,0:T(8,128)(2,1)} %bitcast.33, bf16[16,16,24,1024]{3,2,1,0:T(8,128)(2,1)} %get-tuple-element.5.kv_ref, ...), custom_call_target="tpu_custom_call" | custom-call | tf_op jit(solution)/shard_map/causal/pallas_call | solution.py:455
  109.7 0.7 copy.24
  110.3 3.3 %reshape.44 = bf16[24,16,4096]{2,1,0:T(8,128)(2,1)} reshape(bf16[24,16,4,8,128]{4,3,2,1,0:T(8,128)(2,1)S(1)} %copy.24) | data formatting | bytes 6291456 | tf_op jit(solution)/shard_map/reshape | solution.py:472
  (3 shorter events, 0.0 us)
Async XLA Ops:
  3.0 2.8 %copy-start.3 = (bf16[24,16,4096]{2,1,0:T(8,128)(2,1)S(1)}, bf16[24,16,4096]{2,1,0:T(8,128)(2,1)}, u32[]{:S(2)}) copy-start(bf16[24,16,4096]{2,1,0:T(8,128)(2,1)} %param.10) | copy-start | bytes 9437188
  6.7 5.3 %copy-start.5 = (f32[32]{0:T(128)S(1)}, f32[32]{0:T(128)}, u32[]{:S(2)}) copy-start(f32[32]{0:T(128)} %param.14) | copy-start | bytes 388
  6.7 5.7 %copy-start.2 = (s32[16]{0:T(128)S(1)}, s32[16]{0:T(128)}, u32[]{:S(2)}) copy-start(s32[16]{0:T(128)} %image_ref.1) | copy-start | bytes 196
  12.4 1.6 %copy-start = (bf16[2,2,512,512]{3,2,1,0:T(8,128)(2,1)S(1)}, bf16[2,2,512,512]{3,2,1,0:T(8,128)(2,1)}, u32[]{:S(2)}) copy-start(bf16[2,2,512,512]{3,2,1,0:T(8,128)(2,1)} %cache_ref.1) | copy-start | bytes 6291460
  86.2 2.0 %copy-start.4 = (bf16[24,16,4096]{2,1,0:T(8,128)(2,1)S(1)}, bf16[24,16,4096]{2,1,0:T(8,128)(2,1)}, u32[]{:S(2)}) copy-start(bf16[24,16,4096]{2,1,0:T(8,128)(2,1)} %param.9) | copy-start | bytes 9437188
  89.1 5.3 %copy-start.1 = (s32[16]{0:T(128)S(1)}, s32[16]{0:T(128)}, u32[]{:S(2)}) copy-start(s32[16]{0:T(128)} %lengths_ref.1) | copy-start | bytes 196

commit v3 on v2

--- a/solution.py
+++ b/solution.py
@@ -163,6 +163,9 @@
 
 
 CHUNK = 8
+STEP_US = 1.5
+LINK_BYTES_PER_US = 45000.0
+SCALE_LOG2 = SCALE * math.log2(math.e)
 
 
 def rank_limit(requests, slot, first):
@@ -171,7 +174,7 @@
     return min(requests, (requests * slot // 2 - requests) // first)
 
 
-def relay_plan(chips, requests, slot, step_us):
+def relay_plan(chips, requests, slot, local):
     span = slot // chips
     limit = [rank_limit(requests, slot, span * chip) for chip in range(chips)]
     chunks = [(0, CHUNK), (CHUNK, requests)]
@@ -182,9 +185,12 @@
         return lo, max(lo, min(hi, top))
 
     free = {}
-    pending = [(0.0, chip, chip, "own", chunk) for chip in range(chips) for chunk in range(2)]
+    rate = local * 2048 / LINK_BYTES_PER_US
+    pending = []
+    for chip in range(chips):
+        pending.append((0.0, chip, chip, "own", 0))
+        pending.append((rate * CHUNK * (chip // 2 + 1), chip, chip, "own", 1))
     events = [[] for _ in range(chips)]
-    rate = span // 2 * 2048 / 45000.0
     while pending:
         pending.sort()
         time, chip, source, via, chunk = pending.pop(0)
@@ -205,17 +211,44 @@
                 kept.append((target, lo, hi))
         got = ranks(chip, chunk, via == "up")
         need = ranks(chip, chunk, False)
-        events[chip].append((int(time / step_us), source, via, chunk, got, need, kept))
-    return events
-
-
-def gather_kernel(
-    devices, requests, local, plan, image_ref, picks_ref, query_ref, cache_ref, gate_ref,
-    kv_ref, owned_ref, cross_ref, send_sem, recv_sem, pass_sem, owned_send, owned_recv, local_sem,
+        events[chip].append((time, source, via, chunk, got, need, kept))
+
+    cross_steps, causal_steps = [], []
+    for chip in range(chips):
+        last = max(position for position, event in enumerate(events[chip]) if event[3] == 0)
+        early, late = {}, {}
+        base = max(limit[chip], int(events[chip][last][0] / STEP_US) + 1)
+        for position, event in enumerate(events[chip]):
+            step = int(event[0] / STEP_US)
+            if step < limit[chip]:
+                early.setdefault(step, []).append(position)
+            elif position <= last:
+                late.setdefault(0, []).append(position)
+            else:
+                late.setdefault(max(0, min(CHUNK, step - base)), []).append(position)
+        cross_steps.append(early)
+        causal_steps.append(late)
+    return limit, events, cross_steps, causal_steps
+
+
+def weigh(scores, values):
+    top = jnp.max(scores, axis=-1, keepdims=True)
+    weights = jnp.exp2((scores - top) * SCALE_LOG2)
+    total = jnp.sum(weights, axis=-1, keepdims=True)
+    return jnp.dot(weights.astype(jnp.bfloat16), values, preferred_element_type=jnp.float32), total
+
+
+def relay_kernel(
+    devices, requests, local, slot, plan,
+    order_ref, image_ref, lengths_ref, picks_ref, query_ref, cross_query_ref, cache_ref, gate_ref,
+    out_ref, owned_ref, kv_ref, send_sem, recv_sem, pass_sem, owned_send, owned_recv, local_sem,
 ):
+    limit, events, cross_steps, causal_steps = plan
     me = lax.axis_index("tok")
     chip, core = lax.div(me, 2), lax.rem(me, 2)
-
+    rows = QUERY_PER_KEY * local
+    first = me * local
+    needed = first + local
     barrier = pltpu.get_barrier_semaphore()
 
     def greet(offset, carry):
@@ -229,17 +262,11 @@
 
     keep = pltpu.make_async_copy(picks_ref.at[pl.ds(0, requests)], kv_ref.at[me], local_sem.at[0])
     keep_owned = pltpu.make_async_copy(picks_ref.at[requests + me], owned_ref.at[me], local_sem.at[1])
-    keep.start()
-    keep_owned.start()
-
-    def block(source, lo, hi, own):
-        if own:
-            return picks_ref.at[pl.ds(lo, hi - lo)]
-        return kv_ref.at[source, pl.ds(lo, hi - lo)]
 
     def relay(source, lo, hi, chunk, target, send, own):
+        here = picks_ref.at[pl.ds(lo, hi - lo)] if own else kv_ref.at[source, pl.ds(lo, hi - lo)]
         return pltpu.make_async_remote_copy(
-            src_ref=block(source, lo, hi, own),
+            src_ref=here,
             dst_ref=kv_ref.at[source, pl.ds(lo, hi - lo)],
             send_sem=send,
             recv_sem=recv_sem.at[2 * source + chunk],
@@ -248,7 +275,7 @@
         )
 
     def copies(number, position):
-        _, source_chip, via, chunk, _, need, sends = plan[number][position]
+        _, source_chip, via, chunk, _, need, sends = events[number][position]
         source = 2 * source_chip + core
         result = []
         for index, (target, lo, hi) in enumerate(sends):
@@ -262,12 +289,16 @@
         return result
 
     def handle(number, position):
-        _, source_chip, via, chunk, got, _, _ = plan[number][position]
-        source = 2 * source_chip + core
+        _, source_chip, via, chunk, got, _, _ = events[number][position]
         if via != "own":
-            relay(source, got[0], got[1], chunk, me, pass_sem.at[0], False).wait_recv()
+            relay(2 * source_chip + core, got[0], got[1], chunk, me, pass_sem.at[0], False).wait_recv()
         for copy in copies(number, position):
             copy.start()
+
+    def wait_passed(number, wanted):
+        for _, source_chip, _, chunk, _, need, _ in events[number]:
+            if chunk == wanted and need[1] > need[0]:
+                relay(2 * source_chip + 1 - core, need[0], need[1], chunk, me, pass_sem.at[0], False).wait_recv()
 
     def owned_copy(offset):
         target = lax.rem(me + offset, devices)
@@ -284,44 +315,95 @@
         owned_copy(offset).start()
         return carry
 
-    def step(request, carry):
+    count = limit[0]
+    for number in range(1, devices // 2):
+        count = jnp.where(chip == number, limit[number], count)
+
+    def events_at(steps, step, last):
         for number in range(devices // 2):
             @pl.when(chip == number)
             def _():
-                for when in sorted({event[0] for event in plan[number] if event[0] < requests}):
-                    @pl.when(request == when)
+                for when in sorted(set(steps[number]) | set(last)):
+                    @pl.when(step == when)
                     def _():
-                        for position, event in enumerate(plan[number]):
-                            if event[0] == when:
-                                handle(number, position)
-
-        @pl.when(request == 0)
+                        for position in steps[number].get(when, ()):
+                            handle(number, position)
+                        if when in last:
+                            wait_passed(number, last[when])
+
+    def cross_step(place, carry):
+        events_at(cross_steps, place, {})
+
+        @pl.when(place == 0)
         def _():
-            lax.fori_loop(1, devices, owned_start, 0)
-
+            keep.start()
+            keep_owned.start()
+            lax.fori_loop(devices - me, devices, owned_start, 0)
+
+        request = order_ref[place]
         picture = image_ref[request]
         for group in range(KEY_HEAD_COUNT):
             lanes = slice(group * HEAD_WIDTH, (group + 1) * HEAD_WIDTH)
-            weighted, total = attend(
-                query_ref[request, group], cache_ref[0, picture, :, lanes], cache_ref[1, picture, :, lanes], None
+            scores = lax.dot_general(
+                cross_query_ref[request, group], cache_ref[0, picture, :, lanes], NT, preferred_element_type=jnp.float32
             )
-            cross_ref[request, group] = (weighted * (gate_ref[group] / total)).astype(cross_ref.dtype)
+            weighted, total = weigh(scores, cache_ref[1, picture, :, lanes])
+            out_ref[place, group] = (weighted * (gate_ref[group] / total)).astype(out_ref.dtype)
         return carry
 
-    lax.fori_loop(0, requests, step, 0)
+    lax.fori_loop(0, count, cross_step, 0)
+    keep.wait()
+
+    def run(place, keys):
+        request = order_ref[place]
+        sources = -(-keys // local)
+        row = lax.broadcasted_iota(jnp.int32, (rows, keys), 0)
+        position = first + lax.rem(row, local)
+        key = lax.broadcasted_iota(jnp.int32, (rows, keys), 1)
+        allowed = key <= position
+        alive = position[:, :HEAD_WIDTH] < lengths_ref[request]
+        written = lax.broadcasted_iota(jnp.int32, (keys, HEAD_WIDTH), 0) < needed
+
+        def rows_of(lane_block):
+            lanes = slice(lane_block * HEAD_WIDTH, (lane_block + 1) * HEAD_WIDTH)
+            pieces = kv_ref[:sources, place, :, lanes].astype(jnp.float32)
+            return pieces.reshape(sources * local, HEAD_WIDTH)[:keys]
+
+        for group in range(KEY_HEAD_COUNT):
+            key_rows = rows_of(group).astype(jnp.bfloat16)
+            value_rows = jnp.where(written, rows_of(KEY_HEAD_COUNT + group), 0.0).astype(jnp.bfloat16)
+            scores = lax.dot_general(query_ref[request, group], key_rows, NT, preferred_element_type=jnp.float32)
+            weighted, total = weigh(jnp.where(allowed, scores, -1e30), value_rows)
+            own = (weighted / total).astype(jnp.bfloat16).astype(jnp.float32)
+            combined = own + out_ref[place, group].astype(jnp.float32)
+            out_ref[place, group] = jnp.where(alive, combined, 0.0).astype(out_ref.dtype)
+
+    def causal_step(place, carry):
+        events_at(causal_steps, place, {0: 0, CHUNK: 1})
+
+        @pl.when(place == CHUNK)
+        def _():
+            lax.fori_loop(1, devices - me, owned_start, 0)
+
+        for keys in range(128, slot + 1, 128):
+            @pl.when((needed <= keys) & (needed > keys - 128))
+            def _():
+                run(place, keys)
+
+        return carry
+
+    lax.fori_loop(0, count, causal_step, 0)
+
+    def clear(place, carry):
+        out_ref[place] = jnp.zeros(out_ref.shape[1:], out_ref.dtype)
+        return carry
+
+    lax.fori_loop(count, requests, clear, 0)
 
     for number in range(devices // 2):
         @pl.when(chip == number)
         def _():
-            for position, event in enumerate(plan[number]):
-                if event[0] >= requests:
-                    handle(number, position)
-            for position, event in enumerate(plan[number]):
-                _, source_chip, _, chunk, _, need, _ = event
-                if need[1] > need[0]:
-                    relay(
-                        2 * source_chip + 1 - core, need[0], need[1], chunk, me, pass_sem.at[0], False
-                    ).wait_recv()
+            for position in range(len(events[number])):
                 for copy in copies(number, position):
                     copy.wait_send()
 
@@ -339,53 +421,7 @@
         return carry
 
     lax.fori_loop(1, devices, owned_wait, 0)
-    keep.wait()
     keep_owned.wait()
-
-
-def relayed_causal_kernel(local, slot, lengths_ref, rank_ref, first_ref, query_ref, kv_ref, cross_ref, out_ref):
-    request = pl.program_id(0)
-    first = first_ref[0]
-    length = lengths_ref[request]
-    live = length > first
-    rows = QUERY_PER_KEY * local
-    needed = first + local
-
-    def run(keys):
-        sources = -(-keys // local)
-        row = lax.broadcasted_iota(jnp.int32, (rows, keys), 0)
-        position = first + lax.rem(row, local)
-        key = lax.broadcasted_iota(jnp.int32, (rows, keys), 1)
-        allowed = key <= position
-        alive = position[:, :HEAD_WIDTH] < length
-        written = lax.broadcasted_iota(jnp.int32, (keys, HEAD_WIDTH), 0) < needed
-
-        def rows_of(lane_block):
-            lanes = slice(lane_block * HEAD_WIDTH, (lane_block + 1) * HEAD_WIDTH)
-            pieces = kv_ref[:sources, 0, :, lanes].astype(jnp.float32)
-            return pieces.reshape(sources * local, HEAD_WIDTH)[:keys]
-
-        for group in range(KEY_HEAD_COUNT):
-            key_rows = rows_of(group).astype(jnp.bfloat16)
-            value_rows = jnp.where(written, rows_of(KEY_HEAD_COUNT + group), 0.0).astype(jnp.bfloat16)
-            scores = lax.dot_general(query_ref[0, group], key_rows, NT, preferred_element_type=jnp.float32) * SCALE
-            scores = jnp.where(allowed, scores, -1e30)
-            top = jnp.max(scores, axis=-1, keepdims=True)
-            weights = jnp.exp(scores - top)
-            total = jnp.sum(weights, axis=-1, keepdims=True)
-            weighted = jnp.dot(weights.astype(jnp.bfloat16), value_rows, preferred_element_type=jnp.float32)
-            own = (weighted / total).astype(jnp.bfloat16).astype(jnp.float32)
-            combined = own + cross_ref[0, group].astype(jnp.float32)
-            out_ref[0, group] = jnp.where(alive, combined, 0.0).astype(out_ref.dtype)
-
-    for keys in range(128, slot + 1, 128):
-        @pl.when(live & (needed <= keys) & (needed > keys - 128))
-        def _():
-            run(keys)
-
-    @pl.when(jnp.logical_not(live))
-    def _():
-        out_ref[...] = jnp.zeros_like(out_ref)
 
 
 def relayed(
@@ -427,17 +463,16 @@
     head_shape = jax.ShapeDtypeStruct((requests, KEY_HEAD_COUNT, rows, HEAD_WIDTH), jnp.bfloat16)
     anywhere = pl.BlockSpec(memory_space=pl.ANY)
     vmem = pl.BlockSpec(memory_space=pltpu.VMEM)
-    plan = relay_plan(devices // 2, requests, slot, 1.5)
-    kv_all, owned, cross = pl.pallas_call(
-        functools.partial(gather_kernel, devices, requests, local, plan),
-        in_specs=[pl.BlockSpec(memory_space=pltpu.SMEM), anywhere, vmem, vmem, vmem],
-        out_specs=[anywhere, anywhere, vmem],
-        out_shape=[
-            jax.ShapeDtypeStruct((devices, requests, local, width), jnp.bfloat16),
-            jax.ShapeDtypeStruct((devices, local, width), jnp.bfloat16),
-            head_shape,
-        ],
+    plan = relay_plan(devices // 2, requests, slot, local)
+    order = jnp.sum(ids[:, None] * (length_rank[:, None] == ids[None, :]), axis=0).astype(jnp.int32)
+    smem = pl.BlockSpec(memory_space=pltpu.SMEM)
+    by_rank, owned = pl.pallas_call(
+        functools.partial(relay_kernel, devices, requests, local, slot, plan),
+        in_specs=[smem, smem, smem, vmem, vmem, vmem, vmem, vmem],
+        out_specs=[vmem, anywhere],
+        out_shape=[head_shape, jax.ShapeDtypeStruct((devices, local, width), jnp.bfloat16)],
         scratch_shapes=[
+            pltpu.VMEM((devices, requests, local, width), jnp.bfloat16),
             pltpu.SemaphoreType.DMA((2, devices)),
             pltpu.SemaphoreType.DMA((2 * devices,)),
             pltpu.SemaphoreType.DMA((devices,)),
@@ -448,26 +483,9 @@
         compiler_params=pltpu.CompilerParams(
             collective_id=0, has_side_effects=True, vmem_limit_bytes=VMEM_LIMIT
         ),
-        name="gather_cross",
-    )(image_index, picks, by_head(cross_query_rows), image_cache, gate)
-
-    head_block = pl.BlockSpec((1, KEY_HEAD_COUNT, rows, HEAD_WIDTH), lambda r, *_: (r, 0, 0, 0))
-    attended = pl.pallas_call(
-        functools.partial(relayed_causal_kernel, local, slot),
-        grid_spec=pltpu.PrefetchScalarGridSpec(
-            num_scalar_prefetch=3,
-            grid=(requests,),
-            in_specs=[
-                head_block,
-                pl.BlockSpec((devices, 1, local, width), lambda r, lengths, ranks, first: (0, ranks[r], 0, 0)),
-                head_block,
-            ],
-            out_specs=head_block,
-        ),
-        out_shape=head_shape,
-        compiler_params=pltpu.CompilerParams(vmem_limit_bytes=VMEM_LIMIT),
-        name="causal",
-    )(lengths, length_rank, first, by_head(queries), kv_all, cross)
+        name="relay_attention",
+    )(order, image_index, lengths, picks, by_head(queries), by_head(cross_query_rows), image_cache, gate)
+    attended = jnp.take(by_rank, length_rank, axis=0)
     attended = attended.reshape(requests, KEY_HEAD_COUNT, QUERY_PER_KEY, local, HEAD_WIDTH)
     attended = jnp.transpose(attended, (3, 0, 1, 2, 4)).reshape(local, requests, HQ * HEAD_WIDTH)
 

time: 116 us -> 101 us (0.87); the launches traced: 114 us -> 100 us
  Pallas kernels: 87.5 us -> 70.8 us
  local copies, waits for them, and re-layouts: 19.2 us -> 22.3 us
    pallas_call x2 -> x1, Pallas kernels: 87.5 us -> 70.8 us  [relayed(): pl.pallas_call(functools.partial(relay_kernel, devices, requests, local,...]
    gather x0 -> x1, local copies, waits for them, and re-layouts: none -> 3.04 us  [relayed(): attended = jnp.take(by_rank, length_rank, axis=0)]
where the time goes in v3:
time: 101 us; the launch traced here: 100 us
  Pallas kernels  70.8 us (70%)
  local copies, waits for them, and re-layouts  22.3 us (22%)
  other arithmetic  4.61 us (5%)
  matrix products  1.87 us (2%)
    pallas_call x1, Pallas kernels, relayed(): pl.pallas_call(functools.partial(relay_kernel, devices, requests, local,...  70.8 us
    reshape x2, local copies, waits for them, and re-layouts, by_head(): array.reshape(local, requests, KEY_HEAD_COUNT, QUERY_PER_KEY, HEAD_WIDTH)  10.6 us
    reshape x1, local copies, waits for them, and re-layouts, relayed(): jnp.transpose(attended, (3, 0, 1, 2, 4))  3.31 us
    unnamed x14, local copies, waits for them, and re-layouts  3.29 us
    gather x1, local copies, waits for them, and re-layouts, relayed(): attended = jnp.take(by_rank, length_rank, axis=0)  3.04 us

profile of v3, /device:TPU:31, one launch (start us, length us, event | category | flops | bytes accessed | tf_op | source)
XLA Modules:
  0.0 100.3 jit_solution(11185795365925752745)
XLA Ops:
  0.6 0.9 convert_reduce_fusion
  1.5 1.3 %fusion.8 = (s32[]{:T(128)}, s32[16]{0:T(128)S(1)}) fusion(s32[16]{0:T(128)} %lengths_ref.1, s32[16]{0:T(128)} %param.16, s32[]{:T(128)S(6)} %axis_index.12), kind=kLoop, calls=%fused_computation.26 | loop fusion | flops 63 | bytes 200 | tf_op jit(solution)/shard_map/reduce_sum | solution.py:492
  2.9 0.1 pad_add_fusion
  2.9 0.1 eq.22
  3.0 0.1 fusion.4
  3.1 1.9 %fusion = bf16[32,24,1024]{2,0,1:T(8,128)(2,1)S(1)} fusion(bf16[24,16,512]{2,1,0:T(8,128)(2,1)} %param.12, bf16[24,16,512]{2,1,0:T(8,128)(2,1)} %param.11, pred[32,16]{0,1:T(8,128)(4,1)S(1)} %fusion.4), kind=kOutput, calls=%fused_computation.3 | convolution fusion | flops 26738688 | bytes 2359808 | tf_op jit(solution)/shard_map/sr,lrd->sld/dot_general | solution.py:454
  5.0 0.9 copy.28.picks_ref
  5.8 0.1 select_reduce_fusion.order_ref
  5.9 0.0 copy-done.3
  5.9 0.8 copy.25
  6.8 0.0 copy-start.4
  6.8 5.3 %copy.21 = bf16[24,16,4,8,128]{4,0,3,2,1:T(8,128)(2,1)} copy(bf16[24,16,4,8,128]{4,3,2,1,0:T(8,128)(2,1)S(1)} %bitcast.35) | data formatting | bytes 6291456 | tf_op jit(solution)/shard_map/reshape | solution.py:457
  12.1 0.0 copy-done.4
  12.1 0.8 copy.26
  12.9 0.0 copy-start.5
  13.0 0.0 copy-start.1
  13.0 0.0 copy-start.2
  13.0 5.3 %copy.22 = bf16[24,16,4,8,128]{4,0,3,2,1:T(8,128)(2,1)} copy(bf16[24,16,4,8,128]{4,3,2,1,0:T(8,128)(2,1)S(1)} %bitcast.36) | data formatting | bytes 6291456 | tf_op jit(solution)/shard_map/reshape | solution.py:457
  18.3 0.1 broadcast_in_dim.46
  18.4 0.1 broadcast_in_dim.47
  18.5 0.2 reshape.72.gate_ref
  18.7 0.0 copy-start
  18.7 1.6 %copy-done = bf16[2,2,512,512]{3,2,1,0:T(8,128)(2,1)S(1)} copy-done((bf16[2,2,512,512]{3,2,1,0:T(8,128)(2,1)S(1)}, bf16[2,2,512,512]{3,2,1,0:T(8,128)(2,1)}, u32[]{:S(2)}) %copy-start) | copy-done | bytes 2097176
  20.3 70.8 %relay_attention.1 = (bf16[16,4,192,128]{3,2,1,0:T(8,128)(2,1)}, bf16[16,24,1024]{2,1,0:T(8,128)(2,1)S(1)}) custom-call(s32[16]{0:T(128)S(1)} %select_reduce_fusion.order_ref, s32[16]{0:T(128)S(1)} %copy-done.2, s32[16]{0:T(128)S(1)} %copy-done.1, bf16[32,24,1024]{2,1,0:T(8,128)(2,1)S(1)} %copy.28.picks_ref, bf16[16,4,192,128]{3,2,1,0:T(8,128)(2,1)} %bitcast.37, ...), custom_call_target="tpu_custom_call" | custom-call | tf_op jit(solution)/shard_map/relay_attention/pallas_call | solution.py:469
  91.1 0.7 iota_compare_fusion.3
  91.7 0.2 bitcast_select_fusion
  91.9 0.1 slice_bitcast_fusion.1
  91.9 0.9 maximum_bitcast_fusion
  92.9 3.0 %gather_fusion = bf16[16,4,192,128]{3,2,1,0:T(8,128)(2,1)S(1)} fusion(bf16[16,4,192,128]{3,2,1,0:T(8,128)(2,1)} %get-tuple-element.4, s32[1024]{0:T(1024)S(1)} %pad_clamp_fusion), kind=kCustom, calls=%fused_computation | custom fusion | bytes 6291520 | tf_op jit(solution)/shard_map/jit(_take)/gather | solution.py:488
  96.0 0.4 select_bitcast_fusion
  96.3 0.7 copy.24
  97.0 3.3 %reshape.61 = bf16[24,16,4096]{2,1,0:T(8,128)(2,1)} reshape(bf16[24,16,4,8,128]{4,3,2,1,0:T(8,128)(2,1)S(1)} %copy.24) | data formatting | bytes 6291456 | tf_op jit(solution)/shard_map/reshape | solution.py:490
  (8 shorter events, 0.0 us)
Async XLA Ops:
  3.0 2.9 %copy-start.3 = (bf16[24,16,4096]{2,1,0:T(8,128)(2,1)S(1)}, bf16[24,16,4096]{2,1,0:T(8,128)(2,1)}, u32[]{:S(2)}) copy-start(bf16[24,16,4096]{2,1,0:T(8,128)(2,1)} %param.9) | copy-start | bytes 9437188
  6.8 5.3 %copy-start.4 = (bf16[24,16,4096]{2,1,0:T(8,128)(2,1)S(1)}, bf16[24,16,4096]{2,1,0:T(8,128)(2,1)}, u32[]{:S(2)}) copy-start(bf16[24,16,4096]{2,1,0:T(8,128)(2,1)} %param.10) | copy-start | bytes 9437188
  12.9 5.3 %copy-start.5 = (f32[32]{0:T(128)S(1)}, f32[32]{0:T(128)}, u32[]{:S(2)}) copy-start(f32[32]{0:T(128)} %param.14) | copy-start | bytes 388
  13.0 5.7 %copy-start.1 = (s32[16]{0:T(128)S(1)}, s32[16]{0:T(128)}, u32[]{:S(2)}) copy-start(s32[16]{0:T(128)} %lengths_ref.1) | copy-start | bytes 196
  13.0 5.7 %copy-start.2 = (s32[16]{0:T(128)S(1)}, s32[16]{0:T(128)}, u32[]{:S(2)}) copy-start(s32[16]{0:T(128)} %image_ref.1) | copy-start | bytes 196
  18.7 1.6 %copy-start = (bf16[2,2,512,512]{3,2,1,0:T(8,128)(2,1)S(1)}, bf16[2,2,512,512]{3,2,1,0:T(8,128)(2,1)}, u32[]{:S(2)}) copy-start(bf16[2,2,512,512]{3,2,1,0:T(8,128)(2,1)} %cache_ref.1) | copy-start | bytes 6291460

commit v4 on v3

--- a/solution.py
+++ b/solution.py
@@ -13,7 +13,7 @@
 HEAD_WIDTH = 128
 QUERY_PER_KEY = 8
 SCALE = 1.0 / math.sqrt(HEAD_WIDTH)
-VMEM_LIMIT = 48 * 1024 * 1024
+VMEM_LIMIT = 52 * 1024 * 1024
 
 NT = (((1,), (1,)), ((), ()))
 
@@ -164,6 +164,7 @@
 
 CHUNK = 8
 STEP_US = 1.5
+TURN_STEPS = 8
 LINK_BYTES_PER_US = 45000.0
 SCALE_LOG2 = SCALE * math.log2(math.e)
 
@@ -241,7 +242,7 @@
 def relay_kernel(
     devices, requests, local, slot, plan,
     order_ref, image_ref, lengths_ref, picks_ref, query_ref, cross_query_ref, cache_ref, gate_ref,
-    out_ref, owned_ref, kv_ref, send_sem, recv_sem, pass_sem, owned_send, owned_recv, local_sem,
+    out_ref, owned_ref, kv_ref, turned_ref, turned_cross_ref, send_sem, recv_sem, pass_sem, owned_send, owned_recv, local_sem,
 ):
     limit, events, cross_steps, causal_steps = plan
     me = lax.axis_index("tok")
@@ -331,6 +332,22 @@
                         if when in last:
                             wait_passed(number, last[when])
 
+    def turn(source_ref, target_ref, head):
+        lanes = pl.ds(pl.multiple_of(head * HEAD_WIDTH, HEAD_WIDTH), HEAD_WIDTH)
+        target_ref[:, head] = jnp.swapaxes(source_ref[:, :, lanes].astype(jnp.float32), 0, 1)
+
+    def turn_cross(head, carry):
+        turn(cross_query_ref, turned_cross_ref, head)
+        return carry
+
+    def turn_own(head, carry):
+        turn(query_ref, turned_ref, head)
+        return carry
+
+    def head_rows(turned, request, group):
+        part = turned[request, group * QUERY_PER_KEY : (group + 1) * QUERY_PER_KEY]
+        return part.reshape(rows, HEAD_WIDTH).astype(jnp.bfloat16)
+
     def cross_step(place, carry):
         events_at(cross_steps, place, {})
 
@@ -339,13 +356,18 @@
             keep.start()
             keep_owned.start()
             lax.fori_loop(devices - me, devices, owned_start, 0)
+            lax.fori_loop(0, HQ, turn_cross, 0)
+
+        @pl.when(place < TURN_STEPS)
+        def _():
+            lax.fori_loop(place * (HQ // TURN_STEPS), (place + 1) * (HQ // TURN_STEPS), turn_own, 0)
 
         request = order_ref[place]
         picture = image_ref[request]
         for group in range(KEY_HEAD_COUNT):
             lanes = slice(group * HEAD_WIDTH, (group + 1) * HEAD_WIDTH)
             scores = lax.dot_general(
-                cross_query_ref[request, group], cache_ref[0, picture, :, lanes], NT, preferred_element_type=jnp.float32
+                head_rows(turned_cross_ref, request, group), cache_ref[0, picture, :, lanes], NT, preferred_element_type=jnp.float32
             )
             weighted, total = weigh(scores, cache_ref[1, picture, :, lanes])
             out_ref[place, group] = (weighted * (gate_ref[group] / total)).astype(out_ref.dtype)
@@ -372,7 +394,9 @@
         for group in range(KEY_HEAD_COUNT):
             key_rows = rows_of(group).astype(jnp.bfloat16)
             value_rows = jnp.where(written, rows_of(KEY_HEAD_COUNT + group), 0.0).astype(jnp.bfloat16)
-            scores = lax.dot_general(query_ref[request, group], key_rows, NT, preferred_element_type=jnp.float32)
+            scores = lax.dot_general(
+                head_rows(turned_ref, request, group), key_rows, NT, preferred_element_type=jnp.float32
+            )
             weighted, total = weigh(jnp.where(allowed, scores, -1e30), value_rows)
             own = (weighted / total).astype(jnp.bfloat16).astype(jnp.float32)
             combined = own + out_ref[place, group].astype(jnp.float32)
@@ -453,10 +477,6 @@
     kv = jnp.concatenate([prompt_key_rows, prompt_value_rows], axis=-1)
     picks = jnp.einsum("sr,lrd->sld", pick, kv, preferred_element_type=jnp.float32).astype(jnp.bfloat16)
 
-    def by_head(array):
-        array = array.reshape(local, requests, KEY_HEAD_COUNT, QUERY_PER_KEY, HEAD_WIDTH)
-        return jnp.transpose(array, (1, 2, 3, 0, 4)).reshape(requests, KEY_HEAD_COUNT, rows, HEAD_WIDTH)
-
     gate = jnp.tanh(query_head_gate).reshape(KEY_HEAD_COUNT, QUERY_PER_KEY, 1)
     gate = jnp.broadcast_to(gate, (KEY_HEAD_COUNT, QUERY_PER_KEY, local)).reshape(KEY_HEAD_COUNT, rows, 1)
 
@@ -473,6 +493,8 @@
         out_shape=[head_shape, jax.ShapeDtypeStruct((devices, local, width), jnp.bfloat16)],
         scratch_shapes=[
             pltpu.VMEM((devices, requests, local, width), jnp.bfloat16),
+            pltpu.VMEM((requests, HQ, local, HEAD_WIDTH), jnp.float32),
+            pltpu.VMEM((requests, HQ, local, HEAD_WIDTH), jnp.float32),
             pltpu.SemaphoreType.DMA((2, devices)),
             pltpu.SemaphoreType.DMA((2 * devices,)),
             pltpu.SemaphoreType.DMA((devices,)),
@@ -484,7 +506,7 @@
             collective_id=0, has_side_effects=True, vmem_limit_bytes=VMEM_LIMIT
         ),
         name="relay_attention",
-    )(order, image_index, lengths, picks, by_head(queries), by_head(cross_query_rows), image_cache, gate)
+    )(order, image_index, lengths, picks, queries, cross_query_rows, image_cache, gate)
     attended = jnp.take(by_rank, length_rank, axis=0)
     attended = attended.reshape(requests, KEY_HEAD_COUNT, QUERY_PER_KEY, local, HEAD_WIDTH)
     attended = jnp.transpose(attended, (3, 0, 1, 2, 4)).reshape(local, requests, HQ * HEAD_WIDTH)

time: 101 us -> 89.8 us (0.89)
  local copies, waits for them, and re-layouts: 22.3 us -> 9.51 us
  Pallas kernels: 70.8 us -> 73 us
    reshape x2 -> x0, local copies, waits for them, and re-layouts: 10.6 us -> none  [by_head(): array.reshape(local, requests, KEY_HEAD_COUNT, QUERY_PER_KEY, HEAD_WIDTH)]
    unnamed x14 -> x6, local copies, waits for them, and re-layouts: 3.29 us -> 0.01 us
    pallas_call x1, Pallas kernels: 70.8 us -> 73 us  [relayed(): pl.pallas_call(functools.partial(relay_kernel, devices, requests, local,...]
    dot_general x1, local copies, waits for them, and re-layouts: 0.87 us -> 2.01 us  [relayed(): jnp.einsum('sr,lrd->sld', pick, kv, preferred_element_type=jnp.float32)]
where the time goes in v4:
time: 89.8 us; the launch traced here: 89.6 us
  Pallas kernels  73 us (81%)
  local copies, waits for them, and re-layouts  9.51 us (11%)
  other arithmetic  4.62 us (5%)
  matrix products  1.72 us (2%)
    pallas_call x1, Pallas kernels, relayed(): pl.pallas_call(functools.partial(relay_kernel, devices, requests, local,...  73 us
    reshape x1, local copies, waits for them, and re-layouts, relayed(): jnp.transpose(attended, (3, 0, 1, 2, 4))  3.31 us
    gather x1, local copies, waits for them, and re-layouts, relayed(): attended = jnp.take(by_rank, length_rank, axis=0)  3.04 us
    dot_general x1, local copies, waits for them, and re-layouts, relayed(): jnp.einsum('sr,lrd->sld', pick, kv, preferred_element_type=jnp.float32)  2.01 us

profile of v4, /device:TPU:31, one launch (start us, length us, event | category | flops | bytes accessed | tf_op | source)
XLA Modules:
  0.0 89.6 jit_solution(7589421995881651107)
XLA Ops:
  0.6 0.0 copy-start
  0.6 0.0 copy-start.2
  0.7 0.0 copy-start.1
  0.7 0.9 %convert_reduce_fusion = s32[16]{0:T(128)S(1)} fusion(s32[16]{0:T(128)} %lengths_ref.1), kind=kLoop, calls=%fused_computation.15 | loop fusion | flops 1776 | bytes 128 | tf_op jit(solution)/shard_map/reduce_sum | solution.py:473
  1.6 1.3 %fusion.8 = (s32[]{:T(128)}, s32[16]{0:T(128)S(1)}) fusion(s32[16]{0:T(128)} %lengths_ref.1, s32[16]{0:T(128)} %param.16, s32[]{:T(128)S(6)} %axis_index.12), kind=kLoop, calls=%fused_computation.26 | loop fusion | flops 63 | bytes 200 | tf_op jit(solution)/shard_map/reduce_sum | solution.py:514
  2.9 0.1 pad_add_fusion
  3.0 0.1 eq.22
  3.1 0.1 fusion.4
  3.1 1.7 %fusion = bf16[32,24,1024]{2,0,1:T(8,128)(2,1)S(1)} fusion(bf16[24,16,512]{2,1,0:T(8,128)(2,1)} %param.12, bf16[24,16,512]{2,1,0:T(8,128)(2,1)} %param.11, pred[32,16]{0,1:T(8,128)(4,1)S(1)} %fusion.4), kind=kOutput, calls=%fused_computation.3 | convolution fusion | flops 26738688 | bytes 2359808 | tf_op jit(solution)/shard_map/sr,lrd->sld/dot_general | solution.py:478
  4.9 2.0 %copy.20.picks_ref = bf16[32,24,1024]{2,1,0:T(8,128)(2,1)} copy(bf16[32,24,1024]{2,0,1:T(8,128)(2,1)S(1)} %fusion) | data formatting | bytes 3145728 | tf_op jit(solution)/shard_map/sr,lrd->sld/dot_general | solution.py:478
  6.9 0.1 select_reduce_fusion.order_ref
  7.0 0.0 copy-done.2
  7.0 0.1 broadcast_in_dim.46
  7.0 0.1 broadcast_in_dim.47
  7.1 0.2 reshape.56.gate_ref
  7.3 0.0 copy-done
  7.3 0.0 copy-done.1
  7.3 73.0 %relay_attention.1 = (bf16[16,4,192,128]{3,2,1,0:T(8,128)(2,1)}, bf16[16,24,1024]{2,1,0:T(8,128)(2,1)S(1)}) custom-call(s32[16]{0:T(128)S(1)} %select_reduce_fusion.order_ref, s32[16]{0:T(128)S(1)} %copy-done.1, s32[16]{0:T(128)S(1)} %copy-done, bf16[32,24,1024]{2,1,0:T(8,128)(2,1)} %copy.20.picks_ref, bf16[24,16,4096]{2,1,0:T(8,128)(2,1)} %query_ref.1, ...), custom_call_target="tpu_custom_call" | custom-call | tf_op jit(solution)/shard_map/relay_attention/pallas_call | solution.py:489
  80.4 0.7 iota_compare_fusion.3
  81.0 0.2 bitcast_select_fusion
  81.2 0.1 slice_bitcast_fusion.1
  81.2 0.9 %maximum_bitcast_fusion = bf16[2,1,384,512]{3,2,1,0:T(8,128)(2,1)} fusion(bf16[1,384,512]{2,1,0:T(8,128)(2,1)S(1)} %get-tuple-element.7, bf16[1,384,512]{2,1,0:T(8,128)(2,1)S(1)} %get-tuple-element.6), kind=kLoop, calls=%fused_computation.7 | loop fusion | flops 393216 | bytes 1572864 | tf_op jit(solution)/shard_map/broadcast_in_dim | solution.py:517
  82.2 3.0 %gather_fusion = bf16[16,4,192,128]{3,2,1,0:T(8,128)(2,1)S(1)} fusion(bf16[16,4,192,128]{3,2,1,0:T(8,128)(2,1)} %get-tuple-element.4, s32[1024]{0:T(1024)S(1)} %pad_clamp_fusion), kind=kCustom, calls=%fused_computation | custom fusion | bytes 6291520 | tf_op jit(solution)/shard_map/jit(_take)/gather | solution.py:510
  85.3 0.4 select_bitcast_fusion
  85.6 0.7 copy.18
  86.3 3.3 %reshape.45 = bf16[24,16,4096]{2,1,0:T(8,128)(2,1)} reshape(bf16[24,16,4,8,128]{4,3,2,1,0:T(8,128)(2,1)S(1)} %copy.18) | data formatting | bytes 6291456 | tf_op jit(solution)/shard_map/reshape | solution.py:512
  (4 shorter events, 0.0 us)
Async XLA Ops:
  0.6 6.7 %copy-start = (s32[16]{0:T(128)S(1)}, s32[16]{0:T(128)}, u32[]{:S(2)}) copy-start(s32[16]{0:T(128)} %lengths_ref.1) | copy-start | bytes 196
  0.6 6.3 %copy-start.2 = (f32[32]{0:T(128)S(1)}, f32[32]{0:T(128)}, u32[]{:S(2)}) copy-start(f32[32]{0:T(128)} %param.14) | copy-start | bytes 388
  0.7 6.7 %copy-start.1 = (s32[16]{0:T(128)S(1)}, s32[16]{0:T(128)}, u32[]{:S(2)}) copy-start(s32[16]{0:T(128)} %image_ref.1) | copy-start | bytes 196

commit v5 on v4

--- a/solution.py
+++ b/solution.py
@@ -405,7 +405,7 @@
     def causal_step(place, carry):
         events_at(causal_steps, place, {0: 0, CHUNK: 1})
 
-        @pl.when(place == CHUNK)
+        @pl.when(place == 0)
         def _():
             lax.fori_loop(1, devices - me, owned_start, 0)
 

time: 89.8 us -> 93.7 us (1.043)
  the two profiles are of different devices: /device:TPU:31 before, /device:TPU:25 now
where the time goes in v5:
time: 93.7 us; the launch traced here: 93.5 us
  Pallas kernels  76.9 us (82%)
  local copies, waits for them, and re-layouts  9.51 us (10%)
  other arithmetic  4.62 us (5%)
  matrix products  1.72 us (2%)
    pallas_call x1, Pallas kernels, relayed(): pl.pallas_call(functools.partial(relay_kernel, devices, requests, local,...  76.9 us
    reshape x1, local copies, waits for them, and re-layouts, relayed(): jnp.transpose(attended, (3, 0, 1, 2, 4))  3.31 us
    gather x1, local copies, waits for them, and re-layouts, relayed(): attended = jnp.take(by_rank, length_rank, axis=0)  3.04 us
    dot_general x1, local copies, waits for them, and re-layouts, relayed(): jnp.einsum('sr,lrd->sld', pick, kv, preferred_element_type=jnp.float32)  2.01 us

profile of v5, /device:TPU:25, one launch (start us, length us, event | category | flops | bytes accessed | tf_op | source)
XLA Modules:
  0.0 93.5 jit_solution(6844736282283898530)
XLA Ops:
  0.6 0.0 copy-start
  0.6 0.0 copy-start.2
  0.7 0.0 copy-start.1
  0.7 0.9 convert_reduce_fusion
  1.6 1.3 %fusion.8 = (s32[]{:T(128)}, s32[16]{0:T(128)S(1)}) fusion(s32[16]{0:T(128)} %lengths_ref.1, s32[16]{0:T(128)} %param.16, s32[]{:T(128)S(6)} %axis_index.12), kind=kLoop, calls=%fused_computation.26 | loop fusion | flops 63 | bytes 200 | tf_op jit(solution)/shard_map/reduce_sum | solution.py:514
  2.9 0.1 pad_add_fusion
  3.0 0.1 eq.22
  3.1 0.1 fusion.4
  3.1 1.7 %fusion = bf16[32,24,1024]{2,0,1:T(8,128)(2,1)S(1)} fusion(bf16[24,16,512]{2,1,0:T(8,128)(2,1)} %param.12, bf16[24,16,512]{2,1,0:T(8,128)(2,1)} %param.11, pred[32,16]{0,1:T(8,128)(4,1)S(1)} %fusion.4), kind=kOutput, calls=%fused_computation.3 | convolution fusion | flops 26738688 | bytes 2359808 | tf_op jit(solution)/shard_map/sr,lrd->sld/dot_general | solution.py:478
  4.9 2.0 %copy.20.picks_ref = bf16[32,24,1024]{2,1,0:T(8,128)(2,1)} copy(bf16[32,24,1024]{2,0,1:T(8,128)(2,1)S(1)} %fusion) | data formatting | bytes 3145728 | tf_op jit(solution)/shard_map/sr,lrd->sld/dot_general | solution.py:478
  6.9 0.1 select_reduce_fusion.order_ref
  7.0 0.0 copy-done.2
  7.0 0.1 broadcast_in_dim.46
  7.0 0.1 broadcast_in_dim.47
  7.1 0.2 reshape.56.gate_ref
  7.3 0.0 copy-done
  7.3 0.0 copy-done.1
  7.3 76.9 %relay_attention.1 = (bf16[16,4,192,128]{3,2,1,0:T(8,128)(2,1)}, bf16[16,24,1024]{2,1,0:T(8,128)(2,1)S(1)}) custom-call(s32[16]{0:T(128)S(1)} %select_reduce_fusion.order_ref, s32[16]{0:T(128)S(1)} %copy-done.1, s32[16]{0:T(128)S(1)} %copy-done, bf16[32,24,1024]{2,1,0:T(8,128)(2,1)} %copy.20.picks_ref, bf16[24,16,4096]{2,1,0:T(8,128)(2,1)} %query_ref.1, ...), custom_call_target="tpu_custom_call" | custom-call | tf_op jit(solution)/shard_map/relay_attention/pallas_call | solution.py:489
  84.2 0.7 iota_compare_fusion.3
  84.9 0.2 bitcast_select_fusion
  85.0 0.1 slice_bitcast_fusion.1
  85.1 0.9 %maximum_bitcast_fusion = bf16[2,1,384,512]{3,2,1,0:T(8,128)(2,1)} fusion(bf16[1,384,512]{2,1,0:T(8,128)(2,1)S(1)} %get-tuple-element.7, bf16[1,384,512]{2,1,0:T(8,128)(2,1)S(1)} %get-tuple-element.6), kind=kLoop, calls=%fused_computation.7 | loop fusion | flops 393216 | bytes 1572864 | tf_op jit(solution)/shard_map/broadcast_in_dim | solution.py:517
  86.1 3.0 %gather_fusion = bf16[16,4,192,128]{3,2,1,0:T(8,128)(2,1)S(1)} fusion(bf16[16,4,192,128]{3,2,1,0:T(8,128)(2,1)} %get-tuple-element.4, s32[1024]{0:T(1024)S(1)} %pad_clamp_fusion), kind=kCustom, calls=%fused_computation | custom fusion | bytes 6291520 | tf_op jit(solution)/shard_map/jit(_take)/gather | solution.py:510
  89.1 0.4 select_bitcast_fusion
  89.5 0.7 copy.18
  90.2 3.3 %reshape.45 = bf16[24,16,4096]{2,1,0:T(8,128)(2,1)} reshape(bf16[24,16,4,8,128]{4,3,2,1,0:T(8,128)(2,1)S(1)} %copy.18) | data formatting | bytes 6291456 | tf_op jit(solution)/shard_map/reshape | solution.py:512
  (4 shorter events, 0.0 us)
Async XLA Ops:
  0.6 6.7 %copy-start = (s32[16]{0:T(128)S(1)}, s32[16]{0:T(128)}, u32[]{:S(2)}) copy-start(s32[16]{0:T(128)} %lengths_ref.1) | copy-start | bytes 196
  0.6 6.3 %copy-start.2 = (f32[32]{0:T(128)S(1)}, f32[32]{0:T(128)}, u32[]{:S(2)}) copy-start(f32[32]{0:T(128)} %param.14) | copy-start | bytes 388
  0.7 6.7 %copy-start.1 = (s32[16]{0:T(128)S(1)}, s32[16]{0:T(128)}, u32[]{:S(2)}) copy-start(s32[16]{0:T(128)} %image_ref.1) | copy-start | bytes 196
